TPU v7x, 32 devices: a whole 2x2x4 slice. The times are simulated.
32 devices in a mesh: grp: 8 (over z, x), crm: 4 (over y, core).
Axes of the slice: x: 2, y: 2, z: 4, core: 2. Of those that a mesh axis runs over, the one named last changes fastest.
Arguments:
- crm_state: float32 [1152, 3, 3712], P(('grp', 'crm')), may hold values from -6 to 6
- forcing: float32 [768, 2, 72], P(('grp', 'crm')), may hold values from -6 to 6
- target: int32 [768], P(('grp', 'crm')), may hold values from 0 to 3, as said below
- cost_class: int32 [768], P(('grp', 'crm')), may hold values from 1 to 3
- level_map: float32 [58, 72], replicated, may hold values from 0 to 0.4, as said below
- remap_index: int32 [768, 4], P(('grp', 'crm')), may hold values from 0 to 71, as said below
- remap_weight: float32 [768, 4], P(('grp', 'crm')), may hold values from 0.2 to 1
Outputs:
- new_state: float32 [1152, 3, 3712], P(('grp', 'crm'))
- cloud_water: float32 [768, 3712], P(('grp', 'crm'))
- physics_tendency: float32 [768, 2, 72], P(('grp', 'crm'))
Inputs may be any that keep to these rules, and one draw needn't show every extreme that they name: `target`: of one owner device's columns at most 9 name the same worker; in every group one worker receives exactly 9 columns from each of the group's 4 owners. `remap_index`: entry 0 names a column of the block before the cell's own, entry 1 one of its own block (offset 24), entry 2 one of the block after (offset 2 * 24), entry 3 any of the three. `level_map`: zero except within two GCM levels of the level nearest to each model level.
All inputs are finite; a program needn't handle non-finite values.
Results may differ from a plain program's by a relative error of at most 0.0003.
Values sent between devices are 32-bit elements; how exact they have to be, the bound alone decides.
No kernel may reach another device: no remote copies, remote signals or barrier semaphores. Data moves between devices by JAX's collectives and lax.ppermute only.
A program may use at most 64 MiB of HBM per device.

v0:
```python
import functools

import jax
import jax.numpy as jnp
from jax import lax
from jax.experimental import pallas as pl
from jax.experimental.pallas import tpu as pltpu
from jax.sharding import PartitionSpec as P

CLASSES = 3
SUB = 4
DIFFUSE_HORIZ = 0.2
DIFFUSE_VERT = 0.1
CONDENSE_RATE = 3.0
LINEAR_DRAG = 0.1
MOIST_BUOYANCY = 0.6
HIGHEST = lax.Precision.HIGHEST
F32 = jnp.float32
LANES = 128
ROWS = 8
PHASES = 4
MIB = 1 << 20


def in_hbm(x):
    return pltpu.with_memory_space_constraint(x, pltpu.HBM)


def iota(shape, axis):
    return lax.broadcasted_iota(jnp.int32, shape, axis)


def dot_t(lhs, rhs):
    return lax.dot_general(lhs, rhs, (((0,), (0,)), ((), ())), precision=HIGHEST, preferred_element_type=F32)


def dot(lhs, rhs):
    return jnp.dot(lhs, rhs, precision=HIGHEST, preferred_element_type=F32)


def all_rows(x):
    x = x + pltpu.roll(x, 4, 0)
    x = x + pltpu.roll(x, 2, 0)
    return x + pltpu.roll(x, 1, 0)


def lanes_of(levels):
    base = 2 * levels
    return base, base + 1, base + 2, base + 3


def pack_kernel(capacity, workers, target_hbm, cost_hbm, forcing_hbm, level_hbm, rows, target, cost, forcing, level_map, counts, spread, sems):
    pairs = ((target_hbm, target), (cost_hbm, cost), (forcing_hbm, forcing), (level_hbm, level_map))
    copies = [pltpu.make_async_copy(source, place, sems.at[i]) for i, (source, place) in enumerate(pairs)]
    for copy in copies:
        copy.start()
    for copy in copies:
        copy.wait()
    levels, gcm = level_map.shape
    columns = forcing.shape[0]
    lane_class, lane_slot, lane_column, lane_owner = lanes_of(levels)
    me = lax.axis_index("crm")
    for worker in range(workers):
        counts[worker] = 0
    sub = iota((columns, LANES), 0)
    lane = iota((columns, LANES), 1)
    classes = jnp.zeros((columns, LANES), F32)
    slots = jnp.zeros((columns, LANES), F32)
    for column in range(columns):
        worker = target[column]
        rank = counts[worker]
        counts[worker] = rank + 1
        slot = (worker * workers + me) * capacity + rank
        classes = jnp.where(sub == column, cost[column].astype(F32), classes)
        slots = jnp.where(sub == column, slot.astype(F32), slots)
    spread[...] = jnp.zeros(spread.shape, F32)
    mapped = jnp.zeros((columns, LANES), F32)
    for variable in range(2):
        spread[variable, variable * levels : (variable + 1) * levels, :] = level_map[...]
        mapped = mapped + lax.dot_general(
            forcing[:, variable, :],
            spread[variable],
            (((1,), (1,)), ((), ())),
            precision=HIGHEST,
            preferred_element_type=F32,
        )
    meta = jnp.where(lane == lane_class, classes, 0.0)
    meta = jnp.where(lane == lane_slot, slots, meta)
    meta = jnp.where(lane == lane_column, (sub + 1).astype(F32), meta)
    meta = jnp.where(lane == lane_owner, me.astype(F32), meta)
    rows[...] = jnp.where(lane < lane_class, mapped, meta)


def pack(target, cost, forcing, level_map, workers, capacity):
    columns = forcing.shape[0]
    return pl.pallas_call(
        functools.partial(pack_kernel, capacity, workers),
        out_shape=jax.ShapeDtypeStruct((columns, LANES), F32),
        in_specs=[pl.BlockSpec(memory_space=pl.ANY)] * 4,
        out_specs=pl.BlockSpec(memory_space=pltpu.VMEM),
        scratch_shapes=[
            pltpu.SMEM(target.shape, jnp.int32),
            pltpu.SMEM(cost.shape, jnp.int32),
            pltpu.VMEM(forcing.shape, F32),
            pltpu.VMEM(level_map.shape, F32),
            pltpu.SMEM((workers,), jnp.int32),
            pltpu.VMEM((2, LANES, forcing.shape[2]), F32),
            pltpu.SemaphoreType.DMA((4,)),
        ],
        compiler_params=pltpu.CompilerParams(vmem_limit_bytes=8 * MIB),
        name="pack_forcing",
    )(*(in_hbm(x) for x in (target, cost, forcing, level_map)))


def model_kernel(workers, slots, levels, width, *refs):
    row_refs = refs[:workers]
    x_hbm, fin, xs, t_ref, meta_v, nat, s1, saved, coef, rows_s, meta_s, sem_meta, sem_in = refs[workers:]
    groups = xs.shape[1] // ROWS
    padded = groups * ROWS
    capacity = slots // workers
    tiles = levels * width // LANES
    residues = width // ROWS
    lane_class, lane_slot, lane_column, lane_owner = lanes_of(levels)
    me = lax.axis_index("crm")

    rows = jnp.concatenate([ref[...] for ref in row_refs], axis=0)
    lane_c = iota(rows.shape, 1)
    local = rows[:, lane_slot : lane_slot + 1] - (me * slots).astype(F32)
    member = (local == lane_c.astype(F32)) & (lane_c < slots)
    class_row = jnp.sum(jnp.where(member, rows[:, lane_class : lane_class + 1], 0.0), axis=0, keepdims=True)
    sub_p = iota((padded, LANES), 0)
    lane_p = iota((padded, LANES), 1)
    key_row = class_row * LANES + (LANES - 1 - iota((1, LANES), 1)).astype(F32)
    key_col = jnp.sum(jnp.where(sub_p == lane_p, key_row, 0.0), axis=1, keepdims=True)
    class_col = jnp.sum(jnp.where(sub_p == lane_p, class_row, 0.0), axis=1, keepdims=True)
    ahead_row = ((key_col > key_row) & (sub_p < slots)).astype(F32)
    place_row = jnp.sum(ahead_row, axis=0, keepdims=True)
    ahead_col = ((key_row > key_col) & (lane_p < slots)).astype(F32)
    place_col = jnp.sum(ahead_col, axis=1, keepdims=True)
    here = (place_col == lane_p.astype(F32)) & (sub_p < slots)
    order = jnp.sum(jnp.where(here, sub_p.astype(F32), 0.0), axis=0, keepdims=True)
    class_sorted = jnp.sum(jnp.where(here, class_col, 0.0), axis=0, keepdims=True)
    sub_m = iota((ROWS, LANES), 0)
    lane_m = iota((ROWS, LANES), 1)
    owner_row = jnp.floor((order + 0.5) * (1.0 / capacity))
    rank_row = order - owner_row * capacity
    away_row = owner_row.astype(jnp.int32) ^ me
    table = jnp.where(sub_m == 0, order, jnp.where(sub_m == 1, class_sorted, rank_row)).astype(jnp.int32)
    table = jnp.where(sub_m == 2, away_row, table)
    meta_v[...] = jnp.where(sub_m == 4, place_row.astype(jnp.int32), table)
    fetch = pltpu.make_async_copy(meta_v, meta_s, sem_meta)
    fetch.start()
    fetch.wait()

    def load(index, carry):
        slot = meta_s[0, index]
        pltpu.make_async_copy(x_hbm.at[:, pl.ds(slot, 1), :], xs.at[:, pl.ds(index, 1), :], sem_in.at[index]).start()
        return carry

    lax.fori_loop(0, padded, load, 0, unroll=4)
    place_of = jnp.sum(jnp.where(member, place_row + 1.0, 0.0), axis=1, keepdims=True) - 1.0
    rows_s[...] = dot_t((place_of == lane_c.astype(F32)).astype(F32), rows)[:padded]

    model_of = lax.rem(lane_m, ROWS)
    step_of = lane_m // ROWS
    own = model_of == sub_m

    def coef_index(name, phase=0):
        names = ("a", "bx", "c0", "c1", "aw", "ac")
        return names.index(name) if name in names else len(names) + ("fh", "fq", "fs").index(name) * PHASES + phase

    def at(field, phase, residue):
        return (field * PHASES + phase) * residues + residue

    def substep(src, dst, means, last):
        next_means = []

        def self_at(field, phase, residue):
            return src[at(field, phase, residue)]

        def above(field, phase, residue):
            if phase < PHASES - 1:
                return src[at(field, phase + 1, residue)]
            return pltpu.roll(src[at(field, 0, residue)], LANES - ROWS, 1)

        def below(field, phase, residue):
            if phase > 0:
                return src[at(field, phase - 1, residue)]
            return pltpu.roll(src[at(field, PHASES - 1, residue)], ROWS, 1)

        a, bx, aw, ac = (coef[coef_index(name)] for name in ("a", "bx", "aw", "ac"))
        for phase in range(PHASES):
            c1 = coef[coef_index("c0" if phase < 2 else "c1")]
            fh, fq, fs = (coef[coef_index(name, phase)] for name in ("fh", "fq", "fs"))
            def around(field, residue):
                if residue > 0:
                    left = self_at(field, phase, residue - 1)
                else:
                    left = pltpu.roll(self_at(field, phase, residues - 1), 1, 0)
                if residue < residues - 1:
                    return left + self_at(field, phase, residue + 1)
                return left + pltpu.roll(self_at(field, phase, 0), ROWS - 1, 0)

            pushed = []
            for residue in range(residues):
                wind = self_at(2, phase, residue)
                new_wind = (aw * wind + (self_at(0, phase, residue) - self_at(1, phase, residue))) + bx * around(2, residue)
                new_wind = new_wind + c1 * (above(2, phase, residue) + below(2, phase, residue))
                if not last:
                    dst[at(2, phase, residue)] = new_wind
                pushed.append(new_wind)
            total = pushed
            while len(total) > 1:
                total = [sum(total[i : i + 2]) for i in range(0, len(total), 2)]
            mean = all_rows(total[0]) * (1.0 / width)
            next_means.append(mean)
            if last:
                for residue in range(residues):
                    dst[at(2, phase, residue)] = pushed[residue] - mean
            up_base = c1 if means is None else c1 + means[phase]
            down_base = c1 if means is None else c1 - means[phase]
            for residue in range(residues):
                heat, moist, wind = (self_at(field, phase, residue) for field in range(3))
                up_coef = up_base - wind
                down_coef = down_base + wind
                new_heat = (a * heat + fh) + bx * around(0, residue)
                dst[at(0, phase, residue)] = new_heat + (
                    up_coef * above(0, phase, residue) + down_coef * below(0, phase, residue)
                )
                new_moist = jnp.minimum(a * moist + fq, ac * moist + fs) + bx * around(1, residue)
                dst[at(1, phase, residue)] = new_moist + (
                    up_coef * above(1, phase, residue) + down_coef * below(1, phase, residue)
                )
        return next_means

    def run_group(group, carry):
        base = pl.multiple_of(group * ROWS, ROWS)
        units = meta_s[1, base]
        mixed = meta_s[1, base + ROWS - 1] != units

        for member in range(ROWS):
            index = base + member
            pltpu.make_async_copy(x_hbm.at[:, pl.ds(0, 1), :], xs.at[:, pl.ds(index, 1), :], sem_in.at[index]).wait()

        s0 = fin.at[group]

        @pl.when(units > 0)
        def _():
            mine = rows_s[pl.ds(base, ROWS), :]
            class_m = mine[:, lane_class : lane_class + 1]
            class_l = all_rows(jnp.where(own, class_m, 0.0))
            steps = jnp.maximum(class_l * SUB, 1.0)
            dt = 1.0 / steps
            scale = 0.5 * dt * dt
            moist_weight = 1.0 - MOIST_BUOYANCY
            diffuse = 1.0 - 2.0 * (DIFFUSE_HORIZ + DIFFUSE_VERT) * dt
            coef[coef_index("a")] = diffuse
            coef[coef_index("bx")] = DIFFUSE_HORIZ * dt
            inside = [(PHASES * step_of + phase) < levels for phase in range(PHASES)]
            coef[coef_index("c0")] = jnp.where(inside[1], DIFFUSE_VERT * dt, 0.0)
            coef[coef_index("c1")] = jnp.where(inside[3], DIFFUSE_VERT * dt, 0.0)
            coef[coef_index("aw")] = diffuse - LINEAR_DRAG * dt
            coef[coef_index("ac")] = diffuse - CONDENSE_RATE * dt
            for phase in range(PHASES):
                level = PHASES * step_of + phase
                pick = jnp.minimum(level, levels - 1)
                keep = own & inside[phase]
                force = [
                    all_rows(jnp.where(keep, jnp.take_along_axis(mine, pick + variable * levels, axis=1), 0.0))
                    for variable in range(2)
                ]
                saturated = jnp.where(inside[phase], 1.0 - 2.0 * (level.astype(F32) + 0.5) / levels, 0.0)
                fq = (moist_weight * scale * dt) * force[1]
                coef[coef_index("fh", phase)] = (scale * dt) * (force[0] + force[1])
                coef[coef_index("fq", phase)] = fq
                coef[coef_index("fs", phase)] = fq + (CONDENSE_RATE * moist_weight) * dt * scale * saturated

            zero = jnp.zeros((ROWS, LANES), F32)
            for field in range(3):
                for half in range(2):
                    parts = []
                    for step in range(LANES // ROWS):
                        tile = 2 * step + half
                        parts.append(xs[field, pl.ds(base, ROWS), tile * LANES : (tile + 1) * LANES] if tile < tiles else zero)
                    start = (field * PHASES + 2 * half) * width
                    nat[start : start + LANES, :] = jnp.concatenate(parts, axis=0).T

            def natural(field, phase, residue):
                return pl.ds((field * PHASES + phase) * width + residue, ROWS, stride=residues)

            moist_scale = moist_weight * scale
            wind_scale = 0.5 * dt
            before = []
            for phase in range(PHASES):
                sums = [jnp.zeros((ROWS, LANES), F32)] * 2
                for residue in range(residues):
                    theta, moist, wind = (nat[natural(field, phase, residue), :] for field in range(3))
                    scaled = (scale * (theta + moist), moist_scale * moist, wind_scale * wind)
                    for field in range(3):
                        s0[at(field, phase, residue)] = scaled[field]
                    sums = [sums[variable] + scaled[variable] for variable in range(2)]
                before.append(sums)

            def unit(index, inner):
                means = None
                for step in range(SUB):
                    means = substep(*((s0, s1) if step % 2 == 0 else (s1, s0)), means, step == SUB - 1)

                done = class_l == (index + 1).astype(F32)

                def keep(chunk, kept):
                    for residue in range(residues):
                        entry = chunk * residues + residue
                        saved[entry] = jnp.where(done, s0[entry], saved[entry])
                    return kept

                lax.fori_loop(0, jnp.where(mixed & (index + 1 < units), 3 * PHASES, 0), keep, 0)
                return inner

            lax.fori_loop(0, units, unit, 0)

            last = class_l == units.astype(F32)

            def restore(chunk, kept):
                for residue in range(residues):
                    entry = chunk * residues + residue
                    s0[entry] = jnp.where(last, s0[entry], saved[entry])
                return kept

            lax.fori_loop(0, jnp.where(mixed, 3 * PHASES, 0), restore, 0)
            heat_share = (2.0 / width) * steps * steps
            moist_share = heat_share * (1.0 / moist_weight)
            change = []
            for phase in range(PHASES):
                sums = [-value for value in before[phase]]
                for residue in range(residues):
                    sums = [sums[variable] + s0[at(variable, phase, residue)] for variable in range(2)]
                moist = moist_share * all_rows(sums[1])
                change.append((heat_share * all_rows(sums[0]) - moist, moist))

            active = class_m > 0.0
            second = lane_m >= levels
            level = jnp.where(second, lane_m - levels, lane_m)
            pick = jnp.minimum(level // PHASES * ROWS + sub_m, LANES - 1)
            which = lax.rem(level, PHASES)
            tendency = jnp.zeros((ROWS, LANES), F32)
            for phase in range(PHASES):
                found = [jnp.take_along_axis(change[phase][variable], pick, axis=1) for variable in range(2)]
                tendency = jnp.where(which == phase, jnp.where(second, found[1], found[0]), tendency)
            t_ref[pl.ds(base, ROWS), :] = jnp.where((lane_m < lane_class) & active, tendency, jnp.where(lane_m < lane_class, 0.0, mine))

        @pl.when(units <= 0)
        def _():
            t_ref[pl.ds(base, ROWS), :] = jnp.zeros((ROWS, LANES), F32)

        return carry

    lax.fori_loop(0, groups, run_group, 0)


def turned(fin, nat, group, field, width):
    residues = width // ROWS
    tiles = {}
    for half in range(2):
        for pair in range(2):
            phase = 2 * half + pair
            for residue in range(residues):
                spot = pl.ds(phase * width + residue, ROWS, stride=residues)
                nat[spot, :] = fin[group, (field * PHASES + phase) * residues + residue]
        back = nat[2 * half * width : 2 * half * width + LANES, :].T
        for step in range(LANES // ROWS):
            tiles[2 * step + half] = back[step * ROWS : (step + 1) * ROWS]
    return tiles


def weights_of(t_ref, base, lane_class):
    class_m = t_ref[pl.ds(base, ROWS), lane_class : lane_class + 1]
    steps = jnp.broadcast_to(jnp.maximum(class_m * SUB, 1.0), (ROWS, LANES))
    heat = 2.0 * steps * steps
    return class_m > 0.0, heat, heat * (1.0 / (1.0 - MOIST_BUOYANCY)), 2.0 * steps


def cloud_kernel(levels, width, meta, fin, t_ref, water, cl, nat):
    groups = fin.shape[0]
    tiles = levels * width // LANES
    block = -(-tiles // ROWS) * ROWS
    lane_m = iota((ROWS, LANES), 1)
    lane_class = lanes_of(levels)[0]

    def run_group(group, carry):
        base = pl.multiple_of(group * ROWS, ROWS)

        @pl.when(meta[1, base] > 0)
        def _():
            _, _, moist_weight, _ = weights_of(t_ref, base, lane_class)
            parts = turned(fin, nat, group, 1, width)
            for tile in range(tiles):
                value = moist_weight * parts[tile]
                level = (LANES // width) * tile + lane_m // width
                saturated = 1.0 - 2.0 * (level.astype(F32) + 0.5) / levels
                water[pl.ds(base, ROWS), tile * LANES : (tile + 1) * LANES] = value
                cl[pl.ds(base * block + tile, ROWS, stride=block), :] = jnp.maximum(value - saturated, 0.0)

        return carry

    lax.fori_loop(0, groups, run_group, 0)


def send_kernel(workers, capacity, meta, cl, *outs):
    block = outs[0].shape[0] // capacity
    me = lax.axis_index("crm")
    for distance in range(workers):
        first = (me ^ distance) * capacity
        for rank in range(capacity):
            source = pl.multiple_of(meta[4, first + rank] * block, ROWS)
            outs[distance][rank * block : (rank + 1) * block, :] = cl[pl.ds(source, block), :]


def state_kernel(slots, levels, width, meta, fin, t_ref, water, xs, y_hbm, ys, nat, sems):
    groups = fin.shape[0]
    tiles = levels * width // LANES
    lane_class = lanes_of(levels)[0]

    def run_group(group, carry):
        base = pl.multiple_of(group * ROWS, ROWS)

        @pl.when(meta[1, base] > 0)
        def _():
            active, heat_weight, _, wind_weight = weights_of(t_ref, base, lane_class)
            heats = turned(fin, nat, group, 0, width)
            winds = turned(fin, nat, group, 2, width)
            for tile in range(tiles):
                lanes = slice(tile * LANES, (tile + 1) * LANES)
                moist = water[pl.ds(base, ROWS), lanes]
                values = (heat_weight * heats[tile] - moist, moist, wind_weight * winds[tile])
                for field in range(3):
                    spot = (field, pl.ds(base, ROWS), lanes)
                    ys[spot] = jnp.where(active, values[field], xs[spot])

        def store(source, member, inner):
            index = base + member

            @pl.when(index < slots)
            def _():
                pltpu.make_async_copy(
                    source.at[:, pl.ds(index, 1), :], y_hbm.at[:, pl.ds(meta[0, index], 1), :], sems.at[index]
                ).start()

            return inner

        @pl.when(meta[1, base] > 0)
        def _():
            lax.fori_loop(0, ROWS, functools.partial(store, ys), 0)

        @pl.when(meta[1, base] <= 0)
        def _():
            lax.fori_loop(0, ROWS, functools.partial(store, xs), 0)

        return carry

    lax.fori_loop(0, groups, run_group, 0)
    for index in range(slots):
        pltpu.make_async_copy(ys.at[:, pl.ds(index, 1), :], y_hbm.at[:, pl.ds(0, 1), :], sems.at[index]).wait()


def small(name, mib=8, moved=1 << 20):
    cost = pl.CostEstimate(flops=0, bytes_accessed=moved, transcendentals=0)
    return dict(compiler_params=pltpu.CompilerParams(vmem_limit_bytes=mib * MIB), name=name, cost_estimate=cost)


def run_models(row_blocks, state, levels):
    workers = len(row_blocks)
    _, slots, cells = state.shape
    width = cells // levels
    groups = -(-slots // ROWS)
    padded = groups * ROWS
    vmem = pl.BlockSpec(memory_space=pltpu.VMEM)
    entries = 3 * PHASES * (width // ROWS)
    return pl.pallas_call(
        functools.partial(model_kernel, workers, slots, levels, width),
        out_shape=[
            jax.ShapeDtypeStruct((groups, entries, ROWS, LANES), F32),
            jax.ShapeDtypeStruct((3, padded, cells), F32),
            jax.ShapeDtypeStruct((padded, LANES), F32),
            jax.ShapeDtypeStruct((ROWS, LANES), jnp.int32),
        ],
        in_specs=[vmem] * workers + [pl.BlockSpec(memory_space=pl.ANY)],
        out_specs=[vmem] * 4,
        scratch_shapes=[
            pltpu.VMEM((3 * PHASES * width, LANES), F32),
            pltpu.VMEM((entries, ROWS, LANES), F32),
            pltpu.VMEM((entries, ROWS, LANES), F32),
            pltpu.VMEM((6 + 3 * PHASES, ROWS, LANES), F32),
            pltpu.VMEM((padded, LANES), F32),
            pltpu.SMEM((ROWS, LANES), jnp.int32),
            pltpu.SemaphoreType.DMA,
            pltpu.SemaphoreType.DMA((padded,)),
        ],
        **small("cloud_models", 12, 40 << 20),
    )(*row_blocks, state)


def condensate(cells, levels, meta, fin, tendency):
    padded = fin.shape[0] * ROWS
    width = cells // levels
    vmem = pl.BlockSpec(memory_space=pltpu.VMEM)
    block = -(-(cells // LANES) // ROWS) * ROWS
    return pl.pallas_call(
        functools.partial(cloud_kernel, levels, width),
        out_shape=[jax.ShapeDtypeStruct((padded, cells), F32), jax.ShapeDtypeStruct((padded * block, LANES), F32)],
        in_specs=[pl.BlockSpec(memory_space=pltpu.SMEM), vmem, vmem],
        out_specs=[vmem] * 2,
        scratch_shapes=[pltpu.VMEM((PHASES * width, LANES), F32)],
        **small("condensate", moved=8 << 20),
    )(meta, fin, tendency)


def send_blocks(workers, slots, meta, blocks):
    capacity = slots // workers
    block = blocks.shape[0] // (-(-slots // ROWS) * ROWS)
    vmem = pl.BlockSpec(memory_space=pltpu.VMEM)
    return pl.pallas_call(
        functools.partial(send_kernel, workers, capacity),
        out_shape=[jax.ShapeDtypeStruct((capacity * block, LANES), F32)] * workers,
        in_specs=[pl.BlockSpec(memory_space=pltpu.SMEM), vmem],
        out_specs=[vmem] * workers,
        **small("send_blocks"),
    )(meta, blocks)


def state_rows(slots, levels, meta, fin, tendency, water, start):
    width = fin.shape[1] // (3 * PHASES) * ROWS
    fields, padded, cells = start.shape
    vmem = pl.BlockSpec(memory_space=pltpu.VMEM)
    return pl.pallas_call(
        functools.partial(state_kernel, slots, levels, width),
        out_shape=jax.ShapeDtypeStruct((fields, slots, cells), F32),
        in_specs=[pl.BlockSpec(memory_space=pltpu.SMEM)] + [vmem] * 4,
        out_specs=pl.BlockSpec(memory_space=pl.ANY),
        scratch_shapes=[
            pltpu.VMEM((fields, padded, cells), F32),
            pltpu.VMEM((PHASES * width, LANES), F32),
            pltpu.SemaphoreType.DMA((slots,)),
        ],
        **small("state_rows", moved=12 << 20),
    )(meta, fin, tendency, water, start)


def edge_kernel(levels, columns, workers, *refs):
    t_refs, out = refs[:workers], refs[workers]
    _, _, lane_column, lane_owner = lanes_of(levels)
    me = lax.axis_index("crm")
    wanted = jnp.where(me == 0, workers - 1, 0).astype(F32)
    rows = jnp.concatenate([ref[...] for ref in t_refs], axis=0)
    lane = iota(rows.shape, 1).astype(F32)
    owner = rows[:, lane_owner : lane_owner + 1]
    column = rows[:, lane_column : lane_column + 1]
    select = ((owner == wanted) & (column == lane + 1.0)).astype(F32)
    out[...] = dot_t(select, rows)[:columns]


def share_rows(index, weight):
    rows = weight[...]
    total = jnp.sum(rows, axis=0, keepdims=True)
    return index[...].astype(F32), rows / total


def inner_kernel(levels, columns, workers, *refs):
    t_refs = refs[:workers]
    index, weight, level_map, inner, maps = refs[workers:]
    _, _, lane_column, lane_owner = lanes_of(levels)
    me = lax.axis_index("crm")
    rows = jnp.concatenate([ref[...] for ref in t_refs], axis=0)
    owner = rows[:, lane_owner : lane_owner + 1]
    column = rows[:, lane_column : lane_column + 1]
    block = owner - me.astype(F32) + 1.0
    named = (column > 0.0) & (block >= 0.0) & (block <= 2.0)
    ident = jnp.where(named, block * columns + column - 1.0, -1.0)
    wanted, share = share_rows(index, weight)
    mix = jnp.zeros((rows.shape[0], columns), F32)
    for source in range(index.shape[0]):
        mix = mix + jnp.where(ident == wanted[source : source + 1], share[source : source + 1], 0.0)
    inner[...] = dot_t(mix, rows)
    spread_row = iota((levels, LANES), 0)
    spread_lane = iota((levels, LANES), 1)
    for variable in range(2):
        place = (spread_lane == spread_row + variable * levels).astype(F32)
        maps[variable] = dot_t(place, level_map[...])


def physics_kernel(columns, workers, inner, maps, edge, index, weight, out):
    me = lax.axis_index("crm")
    edge_sub = iota((columns, 1), 0)
    edge_block = jnp.where(me == 0, 0, jnp.where(me == workers - 1, 2, -3))
    ident = (edge_block * columns + edge_sub).astype(F32)
    wanted, share = share_rows(index, weight)
    mix = jnp.zeros((columns, columns), F32)
    for source in range(index.shape[0]):
        mix = mix + jnp.where(ident == wanted[source : source + 1], share[source : source + 1], 0.0)
    mixed = inner[...] + dot_t(mix, jnp.where(edge_block >= 0, edge[...], 0.0))
    for variable in range(2):
        out[:, variable, :] = dot(mixed, maps[variable])


def gather_kernel(columns, capacity, workers, *refs):
    target = refs[0]
    received = refs[1 : workers + 1]
    out, counts, column_of, places = refs[workers + 1 :]
    tiles = out.shape[1] // LANES
    block = -(-tiles // ROWS) * ROWS
    me = lax.axis_index("crm")
    for worker in range(workers):
        counts[worker] = 0
    for entry in range(workers * capacity):
        column_of[entry] = columns
    for column in range(columns):
        worker = target[column]
        rank = counts[worker]
        counts[worker] = rank + 1
        column_of[(worker ^ me) * capacity + rank] = column
    for distance in range(workers):
        for rank in range(capacity):
            place = pl.multiple_of(column_of[distance * capacity + rank] * block, ROWS)
            places[pl.ds(place, block), :] = received[distance][rank * block : (rank + 1) * block, :]
    for base in range(0, columns, ROWS):
        count = min(ROWS, columns - base)
        for tile in range(tiles):
            rows = places[pl.ds(base * block + tile, count, stride=block), :]
            out[base : base + count, tile * LANES : (tile + 1) * LANES] = rows


def exchange(blocks, axis):
    size = lax.axis_size(axis)
    out = [blocks[0]]
    for distance in range(1, size):
        out.append(lax.ppermute(blocks[distance], axis, [(i, i ^ distance) for i in range(size)]))
    return out


def body(crm_state, forcing, target, cost_class, level_map, remap_index, remap_weight):
    workers = lax.axis_size("crm")
    groups = lax.axis_size("grp")
    columns = forcing.shape[0]
    slots, _, cells = crm_state.shape
    capacity = slots // workers
    levels, gcm = level_map.shape
    vmem = pl.BlockSpec(memory_space=pltpu.VMEM)

    rows = pack(target, cost_class, forcing, level_map, workers, capacity)
    row_blocks = exchange([rows] * workers, "crm")
    fin, start, tendency, meta = run_models(row_blocks, in_hbm(crm_state.transpose(1, 0, 2)), levels)
    tendencies = exchange([tendency] * workers, "crm")
    water, blocks = condensate(cells, levels, meta, fin, tendency)
    clouds = send_blocks(workers, slots, meta, blocks)
    tendencies, clouds = lax.optimization_barrier((tendencies, clouds))
    clouds = exchange(clouds, "crm")

    edge = pl.pallas_call(
        functools.partial(edge_kernel, levels, columns, workers),
        out_shape=jax.ShapeDtypeStruct((columns, LANES), F32),
        in_specs=[vmem] * workers,
        out_specs=vmem,
        **small("edge_columns"),
    )(*tendencies)
    pairs = []
    for group in range(groups):
        after = (group + 1) % groups
        pairs.append((group * workers, after * workers))
        pairs.append((after * workers + workers - 1, group * workers + workers - 1))
    edge, meta, tendencies = lax.optimization_barrier((edge, meta, tendencies))
    edge = lax.ppermute(edge, ("grp", "crm"), pairs)
    inner, maps = pl.pallas_call(
        functools.partial(inner_kernel, levels, columns, workers),
        out_shape=[jax.ShapeDtypeStruct((columns, LANES), F32), jax.ShapeDtypeStruct((2, LANES, gcm), F32)],
        in_specs=[vmem] * (workers + 3),
        out_specs=[vmem] * 2,
        **small("inner_blocks"),
    )(*tendencies, remap_index.T, remap_weight.T, level_map)
    state = state_rows(slots, levels, meta, fin, tendency, water, start)
    block = clouds[0].shape[0] // capacity
    cloud_water = pl.pallas_call(
        functools.partial(gather_kernel, columns, capacity, workers),
        out_shape=jax.ShapeDtypeStruct((columns, cells), F32),
        in_specs=[pl.BlockSpec(memory_space=pltpu.SMEM)] + [vmem] * workers,
        out_specs=vmem,
        scratch_shapes=[
            pltpu.SMEM((workers,), jnp.int32),
            pltpu.SMEM((slots,), jnp.int32),
            pltpu.VMEM(((columns + 1) * block, LANES), F32),
        ],
        **small("cloud_rows"),
    )(target, *clouds)
    inner, maps, cloud_water = lax.optimization_barrier((inner, maps, cloud_water))
    physics = pl.pallas_call(
        functools.partial(physics_kernel, columns, workers),
        out_shape=jax.ShapeDtypeStruct((columns, 2, gcm), F32),
        in_specs=[vmem] * 5,
        out_specs=vmem,
        **small("physics_cells"),
    )(inner, maps, edge, remap_index.T, remap_weight.T)
    return state.transpose(1, 0, 2), cloud_water, physics


def solution(mesh):
    wide = P(("grp", "crm"), None, None)
    flat = P(("grp", "crm"), None)
    line = P(("grp", "crm"))
    in_specs = (wide, wide, line, line, P(), flat, flat)
    out_specs = (wide, flat, wide)
    return jax.shard_map(body, mesh=mesh, in_specs=in_specs, out_specs=out_specs, check_vma=False)
```

profile of v0, /device:TPU:5, one launch (start us, length us, event | category | flops | bytes accessed | tf_op | source)
XLA Modules:
  0.0 37.7 jit_solution(345925564692442604)
XLA Ops:
  0.6 1.1 %pack_forcing.1.refs_0_ = f32[24,128]{1,0:T(8,128)S(1)} custom-call(s32[24]{0:T(128)} %refs_0_.1, s32[24]{0:T(128)} %cost_hbm.1, f32[24,2,72]{2,1,0:T(2,128)} %forcing_hbm.1, f32[58,72]{1,0:T(8,128)} %refs_6_.1), custom_call_target="tpu_custom_call" | custom-call | tf_op jit(solution)/shard_map/pack_forcing/pallas_call | solution.py:96
  1.8 0.7 %collective-permute-start = (f32[24,128]{1,0:T(8,128)S(1)}, f32[24,128]{1,0:T(8,128)S(1)}, u32[]{:S(2)}, u32[]{:S(2)}) collective-permute-start(f32[24,128]{1,0:T(8,128)S(1)} %pack_forcing.1.refs_0_), channel_id=1, source_target_pairs={{0,1},{1,0},{2,3},{3,2},{4,5},{5,4},{6,7},{7,6},{8,9},{9,8},{10,11... | collective-permute-start | bytes 36872 | tf_op jit(solution)/shard_map/ppermute | solution.py:636
  2.5 0.0 collective-permute-start.1
  2.5 1.7 %collective-permute-start.2 = (f32[24,128]{1,0:T(8,128)S(1)}, f32[24,128]{1,0:T(8,128)S(1)}, u32[]{:S(2)}, u32[]{:S(2)}) collective-permute-start(f32[24,128]{1,0:T(8,128)S(1)} %pack_forcing.1.refs_0_), channel_id=1, source_target_pairs={{0,3},{1,2},{2,1},{3,0},{4,7},{5,6},{6,5},{7,4},{8,11},{9,10},{10,... | collective-permute-start | bytes 36872 | tf_op jit(solution)/shard_map/ppermute | solution.py:636
  4.2 0.0 collective-permute-done.refs_1_
  4.2 0.8 %collective-permute-done.1.refs_2_ = f32[24,128]{1,0:T(8,128)S(1)} collective-permute-done((f32[24,128]{1,0:T(8,128)S(1)}, f32[24,128]{1,0:T(8,128)S(1)}, u32[]{:S(2)}, u32[]{:S(2)}) %collective-permute-start.1) | collective-permute-done | bytes 12320 | tf_op jit(solution)/shard_map/ppermute | solution.py:636
  5.1 0.8 %collective-permute-done.2.refs_3_ = f32[24,128]{1,0:T(8,128)S(1)} collective-permute-done((f32[24,128]{1,0:T(8,128)S(1)}, f32[24,128]{1,0:T(8,128)S(1)}, u32[]{:S(2)}, u32[]{:S(2)}) %collective-permute-start.2) | collective-permute-done | bytes 12320 | tf_op jit(solution)/shard_map/ppermute | solution.py:636
  5.9 7.9 %cloud_models.1 = (f32[5,96,8,128]{3,2,1,0:T(8,128)S(1)}, f32[3,40,3712]{2,1,0:T(8,128)S(1)}, f32[40,128]{1,0:T(8,128)S(1)}, s32[8,128]{1,0:T(8,128)S(1)}) custom-call(f32[24,128]{1,0:T(8,128)S(1)} %pack_forcing.1.refs_0_, f32[24,128]{1,0:T(8,128)S(1)} %collective-permute-done.refs_1_, f32[24,128]{1,0:T(8,128)S(1)} %collective-permute-done.1.refs_2_, ...), custom_call_target="tpu_custom_call" | custom-call | bytes 41943040 | tf_op jit(solution)/shard_map/cloud_models/pallas_call | solution.py:479
  13.8 0.5 %collective-permute-start.3 = (f32[40,128]{1,0:T(8,128)S(1)}, f32[40,128]{1,0:T(8,128)S(1)}, u32[]{:S(2)}, u32[]{:S(2)}) collective-permute-start(f32[40,128]{1,0:T(8,128)S(1)} %get-tuple-element.47.t_ref.refs_0_), channel_id=1, source_target_pairs={{0,1},{1,0},{2,3},{3,2},{4,5},{5,4},{6,7},{7,6},{8,9},{9,8},{10,11... | collective-permute-start | bytes 61448 | tf_op jit(solution)/shard_map/ppermute | solution.py:636
  14.2 4.3 %collective-permute-start.4 = (f32[40,128]{1,0:T(8,128)S(1)}, f32[40,128]{1,0:T(8,128)S(1)}, u32[]{:S(2)}, u32[]{:S(2)}) collective-permute-start(f32[40,128]{1,0:T(8,128)S(1)} %get-tuple-element.47.t_ref.refs_0_), channel_id=1, source_target_pairs={{0,2},{1,3},{2,0},{3,1},{4,6},{5,7},{6,4},{7,5},{8,10},{9,11},{10,... | collective-permute-start | bytes 61448 | tf_op jit(solution)/shard_map/ppermute | solution.py:636
  18.5 0.3 collective-permute-start.5
  18.9 1.2 %condensate.1 = (f32[40,3712]{1,0:T(8,128)S(1)}, f32[1280,128]{1,0:T(8,128)S(1)}) custom-call(s32[8,128]{1,0:T(8,128)S(1)} %get-tuple-element.44.meta, f32[5,96,8,128]{3,2,1,0:T(8,128)S(1)} %get-tuple-element.34.fin, f32[40,128]{1,0:T(8,128)S(1)} %get-tuple-element.47.t_ref.refs_0_), custom_call_target="tpu_custom_call" | custom-call | bytes 8388608 | tf_op jit(solution)/shard_map/condensate/pallas_call | solution.py:508
  20.1 0.7 %send_blocks.1 = (f32[288,128]{1,0:T(8,128)S(1)}, f32[288,128]{1,0:T(8,128)S(1)}, f32[288,128]{1,0:T(8,128)S(1)}, f32[288,128]{1,0:T(8,128)S(1)}) custom-call(s32[8,128]{1,0:T(8,128)S(1)} %get-tuple-element.44.meta, f32[1280,128]{1,0:T(8,128)S(1)} %get-tuple-element.35.cl), custom_call_target="tpu_custom_call" | custom-call | bytes 1048576 | tf_op jit(solution)/shard_map/send_blocks/pallas_call | solution.py:522
  20.8 0.0 collective-permute-done.3.refs_1_
  20.8 0.0 collective-permute-done.4.refs_2_
  20.8 1.4 %collective-permute-done.5.refs_3_ = f32[40,128]{1,0:T(8,128)S(1)} collective-permute-done((f32[40,128]{1,0:T(8,128)S(1)}, f32[40,128]{1,0:T(8,128)S(1)}, u32[]{:S(2)}, u32[]{:S(2)}) %collective-permute-start.5) | collective-permute-done | bytes 20512 | tf_op jit(solution)/shard_map/ppermute | solution.py:636
  22.2 0.4 %collective-permute-start.6 = (f32[288,128]{1,0:T(8,128)S(1)}, f32[288,128]{1,0:T(8,128)S(1)}, u32[]{:S(2)}, u32[]{:S(2)}) collective-permute-start(f32[288,128]{1,0:T(8,128)S(1)} %get-tuple-element.54), channel_id=1, source_target_pairs={{0,1},{1,0},{2,3},{3,2},{4,5},{5,4},{6,7},{7,6},{8,9},{9,8},{10,11... | collective-permute-start | bytes 442376 | tf_op jit(solution)/shard_map/ppermute | solution.py:636
  22.6 0.4 collective-permute-start.7
  23.0 1.4 %collective-permute-start.8 = (f32[288,128]{1,0:T(8,128)S(1)}, f32[288,128]{1,0:T(8,128)S(1)}, u32[]{:S(2)}, u32[]{:S(2)}) collective-permute-start(f32[288,128]{1,0:T(8,128)S(1)} %get-tuple-element.56), channel_id=1, source_target_pairs={{0,3},{1,2},{2,1},{3,0},{4,7},{5,6},{6,5},{7,4},{8,11},{9,10},{10,... | collective-permute-start | bytes 442376 | tf_op jit(solution)/shard_map/ppermute | solution.py:636
  24.3 0.4 %edge_columns.1 = f32[24,128]{1,0:T(8,128)S(1)} custom-call(f32[40,128]{1,0:T(8,128)S(1)} %get-tuple-element.47.t_ref.refs_0_, f32[40,128]{1,0:T(8,128)S(1)} %collective-permute-done.3.refs_1_, f32[40,128]{1,0:T(8,128)S(1)} %collective-permute-done.4.refs_2_, f32[40,128]{1,0:T(8,128)S(1)} %collective-permute-done.5.refs_3_), custom_call_target="tpu_custom_call" | custom-call | bytes 1048576 | tf_op jit(solution)/shard_map/edge_columns/pallas_call | solution.py:658
  24.8 6.6 %collective-permute-start.9 = (f32[24,128]{1,0:T(8,128)S(1)}, f32[24,128]{1,0:T(8,128)S(1)}, u32[]{:S(2)}, u32[]{:S(2)}) collective-permute-start(f32[24,128]{1,0:T(8,128)S(1)} %edge_columns.1), channel_id=1, source_target_pairs={{0,4},{7,3},{4,8},{11,7},{8,12},{15,11},{12,16},{19,15},{16,20},{2... | collective-permute-start | bytes 36872 | tf_op jit(solution)/shard_map/ppermute | solution.py:671
  31.4 0.0 copy-start
  31.4 0.0 copy-start.1
  31.4 0.0 copy-start.2
  31.4 0.0 copy-start.3
  31.4 2.8 %state_rows.1 = f32[3,36,3712]{2,1,0:T(8,128)} custom-call(s32[8,128]{1,0:T(8,128)S(1)} %get-tuple-element.44.meta, f32[5,96,8,128]{3,2,1,0:T(8,128)S(1)} %get-tuple-element.34.fin, f32[40,128]{1,0:T(8,128)S(1)} %get-tuple-element.47.t_ref.refs_0_, f32[40,3712]{1,0:T(8,128)S(1)} %get-tuple-element.45.water, f32[3,40,3712]{2,1,0:T(8,128)S(1)} %get-tuple-element.46.xs), custom_call_target="tpu_custom_call" | custom-call | bytes 12582912 | tf_op jit(solution)/shard_map/state_rows/pallas_call | solution.py:535
  34.3 0.0 copy-done
  34.3 0.0 copy-done.1
  34.3 0.0 copy-done.2
  34.3 0.6 %inner_blocks.1 = (f32[24,128]{1,0:T(8,128)S(1)}, f32[2,128,72]{2,1,0:T(8,128)S(1)}) custom-call(f32[40,128]{1,0:T(8,128)S(1)} %get-tuple-element.47.t_ref.refs_0_, f32[40,128]{1,0:T(8,128)S(1)} %collective-permute-done.3.refs_1_, f32[40,128]{1,0:T(8,128)S(1)} %collective-permute-done.4.refs_2_, f32[40,128]{1,0:T(8,128)S(1)} %collective-permute-done.5.refs_3_, ...), custom_call_target="tpu_custom_call" | custom-call | bytes 1048576 | tf_op jit(solution)/shard_map/inner_blocks/pallas_call | solution.py:672
  34.9 0.0 collective-permute-done.6.refs_2_
  34.9 0.0 collective-permute-done.7.refs_3_
  34.9 0.0 collective-permute-done.8.refs_4_
  34.9 0.0 copy-done.3
  34.9 1.7 %cloud_rows.1 = f32[24,3712]{1,0:T(8,128)} custom-call(s32[24]{0:T(128)S(1)} %copy-done.3, f32[288,128]{1,0:T(8,128)S(1)} %get-tuple-element.53.refs_1_, f32[288,128]{1,0:T(8,128)S(1)} %collective-permute-done.6.refs_2_, f32[288,128]{1,0:T(8,128)S(1)} %collective-permute-done.7.refs_3_, f32[288,128]{1,0:T(8,128)S(1)} %collective-permute-done.8.refs_4_), custom_call_target="tpu_custom_call" | custom-call | bytes 1048576 | tf_op jit(solution)/shard_map/cloud_rows/pallas_call | solution.py:681
  36.6 0.0 collective-permute-done.9.edge
  36.6 1.1 %physics_cells.1 = f32[24,2,72]{2,1,0:T(2,128)} custom-call(f32[24,128]{1,0:T(8,128)S(1)} %get-tuple-element.58.inner, f32[2,128,72]{2,1,0:T(8,128)S(1)} %get-tuple-element.59.maps, f32[24,128]{1,0:T(8,128)S(1)} %collective-permute-done.9.edge, s32[4,24]{1,0:T(4,128)S(1)} %bitcast.5, f32[4,24]{1,0:T(4,128)S(1)} %bitcast.7), custom_call_target="tpu_custom_call" | custom-call | bytes 1048576 | tf_op jit(solution)/shard_map/physics_cells/pallas_call | solution.py:694
Async XLA Ops:
  1.8 2.5 %collective-permute-start = (f32[24,128]{1,0:T(8,128)S(1)}, f32[24,128]{1,0:T(8,128)S(1)}, u32[]{:S(2)}, u32[]{:S(2)}) collective-permute-start(f32[24,128]{1,0:T(8,128)S(1)} %pack_forcing.1.refs_0_), channel_id=1, source_target_pairs={{0,1},{1,0},{2,3},{3,2},{4,5},{5,4},{6,7},{7,6},{8,9},{9,8},{10,11... | collective-permute-start | bytes 36872 | tf_op jit(solution)/shard_map/ppermute | solution.py:636
  2.5 2.6 %collective-permute-start.1 = (f32[24,128]{1,0:T(8,128)S(1)}, f32[24,128]{1,0:T(8,128)S(1)}, u32[]{:S(2)}, u32[]{:S(2)}) collective-permute-start(f32[24,128]{1,0:T(8,128)S(1)} %pack_forcing.1.refs_0_), channel_id=1, source_target_pairs={{0,2},{1,3},{2,0},{3,1},{4,6},{5,7},{6,4},{7,5},{8,10},{9,11},{10,... | collective-permute-start | bytes 36872 | tf_op jit(solution)/shard_map/ppermute | solution.py:636
  2.5 3.4 %collective-permute-start.2 = (f32[24,128]{1,0:T(8,128)S(1)}, f32[24,128]{1,0:T(8,128)S(1)}, u32[]{:S(2)}, u32[]{:S(2)}) collective-permute-start(f32[24,128]{1,0:T(8,128)S(1)} %pack_forcing.1.refs_0_), channel_id=1, source_target_pairs={{0,3},{1,2},{2,1},{3,0},{4,7},{5,6},{6,5},{7,4},{8,11},{9,10},{10,... | collective-permute-start | bytes 36872 | tf_op jit(solution)/shard_map/ppermute | solution.py:636
  13.8 7.0 %collective-permute-start.3 = (f32[40,128]{1,0:T(8,128)S(1)}, f32[40,128]{1,0:T(8,128)S(1)}, u32[]{:S(2)}, u32[]{:S(2)}) collective-permute-start(f32[40,128]{1,0:T(8,128)S(1)} %get-tuple-element.47.t_ref.refs_0_), channel_id=1, source_target_pairs={{0,1},{1,0},{2,3},{3,2},{4,5},{5,4},{6,7},{7,6},{8,9},{9,8},{10,11... | collective-permute-start | bytes 61448 | tf_op jit(solution)/shard_map/ppermute | solution.py:636
  14.2 6.5 %collective-permute-start.4 = (f32[40,128]{1,0:T(8,128)S(1)}, f32[40,128]{1,0:T(8,128)S(1)}, u32[]{:S(2)}, u32[]{:S(2)}) collective-permute-start(f32[40,128]{1,0:T(8,128)S(1)} %get-tuple-element.47.t_ref.refs_0_), channel_id=1, source_target_pairs={{0,2},{1,3},{2,0},{3,1},{4,6},{5,7},{6,4},{7,5},{8,10},{9,11},{10,... | collective-permute-start | bytes 61448 | tf_op jit(solution)/shard_map/ppermute | solution.py:636
  18.5 3.7 %collective-permute-start.5 = (f32[40,128]{1,0:T(8,128)S(1)}, f32[40,128]{1,0:T(8,128)S(1)}, u32[]{:S(2)}, u32[]{:S(2)}) collective-permute-start(f32[40,128]{1,0:T(8,128)S(1)} %get-tuple-element.47.t_ref.refs_0_), channel_id=1, source_target_pairs={{0,3},{1,2},{2,1},{3,0},{4,7},{5,6},{6,5},{7,4},{8,11},{9,10},{10,... | collective-permute-start | bytes 61448 | tf_op jit(solution)/shard_map/ppermute | solution.py:636
  22.2 12.7 %collective-permute-start.6 = (f32[288,128]{1,0:T(8,128)S(1)}, f32[288,128]{1,0:T(8,128)S(1)}, u32[]{:S(2)}, u32[]{:S(2)}) collective-permute-start(f32[288,128]{1,0:T(8,128)S(1)} %get-tuple-element.54), channel_id=1, source_target_pairs={{0,1},{1,0},{2,3},{3,2},{4,5},{5,4},{6,7},{7,6},{8,9},{9,8},{10,11... | collective-permute-start | bytes 442376 | tf_op jit(solution)/shard_map/ppermute | solution.py:636
  22.6 12.3 %collective-permute-start.7 = (f32[288,128]{1,0:T(8,128)S(1)}, f32[288,128]{1,0:T(8,128)S(1)}, u32[]{:S(2)}, u32[]{:S(2)}) collective-permute-start(f32[288,128]{1,0:T(8,128)S(1)} %get-tuple-element.55), channel_id=1, source_target_pairs={{0,2},{1,3},{2,0},{3,1},{4,6},{5,7},{6,4},{7,5},{8,10},{9,11},{10,... | collective-permute-start | bytes 442376 | tf_op jit(solution)/shard_map/ppermute | solution.py:636
  23.0 11.9 %collective-permute-start.8 = (f32[288,128]{1,0:T(8,128)S(1)}, f32[288,128]{1,0:T(8,128)S(1)}, u32[]{:S(2)}, u32[]{:S(2)}) collective-permute-start(f32[288,128]{1,0:T(8,128)S(1)} %get-tuple-element.56), channel_id=1, source_target_pairs={{0,3},{1,2},{2,1},{3,0},{4,7},{5,6},{6,5},{7,4},{8,11},{9,10},{10,... | collective-permute-start | bytes 442376 | tf_op jit(solution)/shard_map/ppermute | solution.py:636
  24.8 11.8 %collective-permute-start.9 = (f32[24,128]{1,0:T(8,128)S(1)}, f32[24,128]{1,0:T(8,128)S(1)}, u32[]{:S(2)}, u32[]{:S(2)}) collective-permute-start(f32[24,128]{1,0:T(8,128)S(1)} %edge_columns.1), channel_id=1, source_target_pairs={{0,4},{7,3},{4,8},{11,7},{8,12},{15,11},{12,16},{19,15},{16,20},{2... | collective-permute-start | bytes 36872 | tf_op jit(solution)/shard_map/ppermute | solution.py:671
  31.4 2.9 %copy-start = (f32[58,72]{1,0:T(8,128)S(1)}, f32[58,72]{1,0:T(8,128)}, u32[]{:S(2)}) copy-start(f32[58,72]{1,0:T(8,128)} %refs_6_.1) | copy-start | bytes 50116
  31.4 2.9 %copy-start.1 = (s32[24,4]{0,1:T(4,128)S(1)}, s32[24,4]{0,1:T(4,128)}, u32[]{:S(2)}) copy-start(s32[24,4]{0,1:T(4,128)} %param.12) | copy-start | bytes 1156
  31.4 2.9 %copy-start.2 = (f32[24,4]{0,1:T(4,128)S(1)}, f32[24,4]{0,1:T(4,128)}, u32[]{:S(2)}) copy-start(f32[24,4]{0,1:T(4,128)} %param.13) | copy-start | bytes 1156
  31.4 3.5 %copy-start.3 = (s32[24]{0:T(128)S(1)}, s32[24]{0:T(128)}, u32[]{:S(2)}) copy-start(s32[24]{0:T(128)} %refs_0_.1) | copy-start | bytes 292
where the time goes:
time: 37.3 us; the launch traced here: 37.7 us
  Pallas kernels  17.4 us (47%)
  starting transfers between devices  16.3 us (44%)
  waiting for transfers between devices  3.1 us (8%)
  between operations  0.8 us (2%)
    ppermute x9, starting transfers between devices, exchange(): lax.ppermute(blocks[distance], axis, [(i, i ^ distance) for i in range(si...  9.68 us
    pallas_call x1, Pallas kernels, run_models(): pl.pallas_call(functools.partial(model_kernel, workers, slots, levels, wi...  7.86 us
    ppermute x1, starting transfers between devices, body(): edge = lax.ppermute(edge, ('grp', 'crm'), pairs)  6.63 us
    ppermute x9, waiting for transfers between devices, exchange(): lax.ppermute(blocks[distance], axis, [(i, i ^ distance) for i in range(si...  3.1 us
    pallas_call x1, Pallas kernels, state_rows(): pl.pallas_call(functools.partial(state_kernel, slots, levels, width), out...  2.82 us
    pallas_call x1, Pallas kernels, body(): pl.pallas_call(functools.partial(gather_kernel, columns, capacity, worker...  1.66 us
    pallas_call x1, Pallas kernels, condensate(): pl.pallas_call(functools.partial(cloud_kernel, levels, width), out_shape=...  1.19 us
    pallas_call x1, Pallas kernels, pack(): pl.pallas_call(functools.partial(pack_kernel, capacity, workers), out_sha...  1.15 us
  transfers between devices with their start and end apart: 10, of which 3 were waited for; matrix products, arithmetic and copies ran while one was open for 0% of the time, Pallas kernels for 20%

commit v1 on v0

--- a/solution.py
+++ b/solution.py
@@ -380,35 +380,24 @@
     return class_m > 0.0, heat, heat * (1.0 / (1.0 - MOIST_BUOYANCY)), 2.0 * steps
 
 
-def cloud_kernel(levels, width, meta, fin, t_ref, water, cl, nat):
-    groups = fin.shape[0]
+def cloud_kernel(levels, width, workers, capacity, meta, fin, t_ref, water, *refs):
+    outs = refs[:workers]
+    cl, nat = refs[workers:]
     tiles = levels * width // LANES
-    block = -(-tiles // ROWS) * ROWS
+    block = outs[0].shape[0] // capacity
     lane_m = iota((ROWS, LANES), 1)
     lane_class = lanes_of(levels)[0]
-
-    def run_group(group, carry):
-        base = pl.multiple_of(group * ROWS, ROWS)
-
-        @pl.when(meta[1, base] > 0)
-        def _():
-            _, _, moist_weight, _ = weights_of(t_ref, base, lane_class)
-            parts = turned(fin, nat, group, 1, width)
-            for tile in range(tiles):
-                value = moist_weight * parts[tile]
-                level = (LANES // width) * tile + lane_m // width
-                saturated = 1.0 - 2.0 * (level.astype(F32) + 0.5) / levels
-                water[pl.ds(base, ROWS), tile * LANES : (tile + 1) * LANES] = value
-                cl[pl.ds(base * block + tile, ROWS, stride=block), :] = jnp.maximum(value - saturated, 0.0)
-
-        return carry
-
-    lax.fori_loop(0, groups, run_group, 0)
-
-
-def send_kernel(workers, capacity, meta, cl, *outs):
-    block = outs[0].shape[0] // capacity
     me = lax.axis_index("crm")
+    for group in range(fin.shape[0]):
+        base = group * ROWS
+        _, _, moist_weight, _ = weights_of(t_ref, base, lane_class)
+        parts = turned(fin, nat.at[group], group, 1, width)
+        for tile in range(tiles):
+            value = moist_weight * parts[tile]
+            level = (LANES // width) * tile + lane_m // width
+            saturated = 1.0 - 2.0 * (level.astype(F32) + 0.5) / levels
+            water[base : base + ROWS, tile * LANES : (tile + 1) * LANES] = value
+            cl[pl.ds(base * block + tile, ROWS, stride=block), :] = jnp.maximum(value - saturated, 0.0)
     for distance in range(workers):
         first = (me ^ distance) * capacity
         for rank in range(capacity):
@@ -416,51 +405,33 @@
             outs[distance][rank * block : (rank + 1) * block, :] = cl[pl.ds(source, block), :]
 
 
-def state_kernel(slots, levels, width, meta, fin, t_ref, water, xs, y_hbm, ys, nat, sems):
+def state_kernel(slots, levels, width, columns, workers, meta, fin, t_ref, water, xs, *refs):
+    inner_refs = refs[: workers + 3]
+    y_hbm, inner, maps, ys, nat, sems = refs[workers + 3 :]
     groups = fin.shape[0]
     tiles = levels * width // LANES
     lane_class = lanes_of(levels)[0]
-
-    def run_group(group, carry):
-        base = pl.multiple_of(group * ROWS, ROWS)
-
-        @pl.when(meta[1, base] > 0)
-        def _():
-            active, heat_weight, _, wind_weight = weights_of(t_ref, base, lane_class)
-            heats = turned(fin, nat, group, 0, width)
-            winds = turned(fin, nat, group, 2, width)
-            for tile in range(tiles):
-                lanes = slice(tile * LANES, (tile + 1) * LANES)
-                moist = water[pl.ds(base, ROWS), lanes]
-                values = (heat_weight * heats[tile] - moist, moist, wind_weight * winds[tile])
-                for field in range(3):
-                    spot = (field, pl.ds(base, ROWS), lanes)
-                    ys[spot] = jnp.where(active, values[field], xs[spot])
-
-        def store(source, member, inner):
-            index = base + member
-
-            @pl.when(index < slots)
-            def _():
-                pltpu.make_async_copy(
-                    source.at[:, pl.ds(index, 1), :], y_hbm.at[:, pl.ds(meta[0, index], 1), :], sems.at[index]
-                ).start()
-
-            return inner
-
-        @pl.when(meta[1, base] > 0)
-        def _():
-            lax.fori_loop(0, ROWS, functools.partial(store, ys), 0)
-
-        @pl.when(meta[1, base] <= 0)
-        def _():
-            lax.fori_loop(0, ROWS, functools.partial(store, xs), 0)
-
-        return carry
-
-    lax.fori_loop(0, groups, run_group, 0)
-    for index in range(slots):
-        pltpu.make_async_copy(ys.at[:, pl.ds(index, 1), :], y_hbm.at[:, pl.ds(0, 1), :], sems.at[index]).wait()
+    copies = []
+    for group in range(groups):
+        base = group * ROWS
+        active, heat_weight, _, wind_weight = weights_of(t_ref, base, lane_class)
+        heats = turned(fin, nat.at[2 * group], group, 0, width)
+        winds = turned(fin, nat.at[2 * group + 1], group, 2, width)
+        for tile in range(tiles):
+            lanes = slice(tile * LANES, (tile + 1) * LANES)
+            moist = water[base : base + ROWS, lanes]
+            values = (heat_weight * heats[tile] - moist, moist, wind_weight * winds[tile])
+            for field in range(3):
+                ys[field, base : base + ROWS, lanes] = jnp.where(active, values[field], xs[field, base : base + ROWS, lanes])
+        for index in range(base, min(base + ROWS, slots)):
+            copy = pltpu.make_async_copy(
+                ys.at[:, pl.ds(index, 1), :], y_hbm.at[:, pl.ds(meta[0, index], 1), :], sems.at[index]
+            )
+            copy.start()
+            copies.append(copy)
+    inner_blocks(levels, columns, workers, *inner_refs, inner, maps)
+    for copy in copies:
+        copy.wait()
 
 
 def small(name, mib=8, moved=1 << 20):
@@ -500,50 +471,46 @@
     )(*row_blocks, state)
 
 
-def condensate(cells, levels, meta, fin, tendency):
-    padded = fin.shape[0] * ROWS
+def condensate(workers, slots, cells, levels, meta, fin, tendency):
+    groups = fin.shape[0]
+    padded = groups * ROWS
     width = cells // levels
+    capacity = slots // workers
     vmem = pl.BlockSpec(memory_space=pltpu.VMEM)
     block = -(-(cells // LANES) // ROWS) * ROWS
-    return pl.pallas_call(
-        functools.partial(cloud_kernel, levels, width),
-        out_shape=[jax.ShapeDtypeStruct((padded, cells), F32), jax.ShapeDtypeStruct((padded * block, LANES), F32)],
+    outs = pl.pallas_call(
+        functools.partial(cloud_kernel, levels, width, workers, capacity),
+        out_shape=[jax.ShapeDtypeStruct((padded, cells), F32)]
+        + [jax.ShapeDtypeStruct((capacity * block, LANES), F32)] * workers,
         in_specs=[pl.BlockSpec(memory_space=pltpu.SMEM), vmem, vmem],
-        out_specs=[vmem] * 2,
-        scratch_shapes=[pltpu.VMEM((PHASES * width, LANES), F32)],
+        out_specs=[vmem] * (workers + 1),
+        scratch_shapes=[pltpu.VMEM((padded * block, LANES), F32), pltpu.VMEM((groups, PHASES * width, LANES), F32)],
         **small("condensate", moved=8 << 20),
     )(meta, fin, tendency)
-
-
-def send_blocks(workers, slots, meta, blocks):
-    capacity = slots // workers
-    block = blocks.shape[0] // (-(-slots // ROWS) * ROWS)
-    vmem = pl.BlockSpec(memory_space=pltpu.VMEM)
-    return pl.pallas_call(
-        functools.partial(send_kernel, workers, capacity),
-        out_shape=[jax.ShapeDtypeStruct((capacity * block, LANES), F32)] * workers,
-        in_specs=[pl.BlockSpec(memory_space=pltpu.SMEM), vmem],
-        out_specs=[vmem] * workers,
-        **small("send_blocks"),
-    )(meta, blocks)
-
-
-def state_rows(slots, levels, meta, fin, tendency, water, start):
+    return outs[0], outs[1:]
+
+
+def state_rows(slots, levels, columns, meta, fin, tendency, water, start, tendencies, index, weight, level_map):
     width = fin.shape[1] // (3 * PHASES) * ROWS
     fields, padded, cells = start.shape
     vmem = pl.BlockSpec(memory_space=pltpu.VMEM)
+    workers = len(tendencies)
     return pl.pallas_call(
-        functools.partial(state_kernel, slots, levels, width),
-        out_shape=jax.ShapeDtypeStruct((fields, slots, cells), F32),
-        in_specs=[pl.BlockSpec(memory_space=pltpu.SMEM)] + [vmem] * 4,
-        out_specs=pl.BlockSpec(memory_space=pl.ANY),
+        functools.partial(state_kernel, slots, levels, width, columns, workers),
+        out_shape=[
+            jax.ShapeDtypeStruct((fields, slots, cells), F32),
+            jax.ShapeDtypeStruct((columns, LANES), F32),
+            jax.ShapeDtypeStruct((2, LANES, level_map.shape[1]), F32),
+        ],
+        in_specs=[pl.BlockSpec(memory_space=pltpu.SMEM)] + [vmem] * (workers + 7),
+        out_specs=[pl.BlockSpec(memory_space=pl.ANY), vmem, vmem],
         scratch_shapes=[
             pltpu.VMEM((fields, padded, cells), F32),
-            pltpu.VMEM((PHASES * width, LANES), F32),
+            pltpu.VMEM((2 * fin.shape[0], PHASES * width, LANES), F32),
             pltpu.SemaphoreType.DMA((slots,)),
         ],
-        **small("state_rows", moved=12 << 20),
-    )(meta, fin, tendency, water, start)
+        **small("state_rows", 12, moved=12 << 20),
+    )(meta, fin, tendency, water, start, *tendencies, index, weight, level_map)
 
 
 def edge_kernel(levels, columns, workers, *refs):
@@ -565,7 +532,7 @@
     return index[...].astype(F32), rows / total
 
 
-def inner_kernel(levels, columns, workers, *refs):
+def inner_blocks(levels, columns, workers, *refs):
     t_refs = refs[:workers]
     index, weight, level_map, inner, maps = refs[workers:]
     _, _, lane_column, lane_owner = lanes_of(levels)
@@ -650,8 +617,7 @@
     row_blocks = exchange([rows] * workers, "crm")
     fin, start, tendency, meta = run_models(row_blocks, in_hbm(crm_state.transpose(1, 0, 2)), levels)
     tendencies = exchange([tendency] * workers, "crm")
-    water, blocks = condensate(cells, levels, meta, fin, tendency)
-    clouds = send_blocks(workers, slots, meta, blocks)
+    water, clouds = condensate(workers, slots, cells, levels, meta, fin, tendency)
     tendencies, clouds = lax.optimization_barrier((tendencies, clouds))
     clouds = exchange(clouds, "crm")
 
@@ -669,14 +635,9 @@
         pairs.append((after * workers + workers - 1, group * workers + workers - 1))
     edge, meta, tendencies = lax.optimization_barrier((edge, meta, tendencies))
     edge = lax.ppermute(edge, ("grp", "crm"), pairs)
-    inner, maps = pl.pallas_call(
-        functools.partial(inner_kernel, levels, columns, workers),
-        out_shape=[jax.ShapeDtypeStruct((columns, LANES), F32), jax.ShapeDtypeStruct((2, LANES, gcm), F32)],
-        in_specs=[vmem] * (workers + 3),
-        out_specs=[vmem] * 2,
-        **small("inner_blocks"),
-    )(*tendencies, remap_index.T, remap_weight.T, level_map)
-    state = state_rows(slots, levels, meta, fin, tendency, water, start)
+    state, inner, maps = state_rows(
+        slots, levels, columns, meta, fin, tendency, water, start, tendencies, remap_index.T, remap_weight.T, level_map
+    )
     block = clouds[0].shape[0] // capacity
     cloud_water = pl.pallas_call(
         functools.partial(gather_kernel, columns, capacity, workers),

time: 37.3 us -> 37.1 us (level)
  Pallas kernels: 17.4 us -> 20.1 us
  starting transfers between devices: 16.3 us -> 14 us
  waiting for transfers between devices: 3.1 us -> 2.21 us
    pallas_call x1, Pallas kernels: 7.86 us -> 11.9 us  [run_models(): pl.pallas_call(functools.partial(model_kernel, workers, slots, levels, wi...]
    ppermute x9, starting transfers between devices: 9.68 us -> 6.78 us  [exchange(): lax.ppermute(blocks[distance], axis, [(i, i ^ distance) for i in range(si...]
    pallas_call x4 -> x2, Pallas kernels: 5.29 us -> 3.87 us  [the longest x1 2.67 us: state_rows(): pl.pallas_call(functools.partial(state_kernel, slots, levels, width, colu...]
    ppermute x9, waiting for transfers between devices: 3.1 us -> 2.2 us  [exchange(): lax.ppermute(blocks[distance], axis, [(i, i ^ distance) for i in range(si...]
    ppermute x1, starting transfers between devices: 6.63 us -> 7.25 us  [body(): edge = lax.ppermute(edge, ('grp', 'crm'), pairs)]
  transfers between devices with their start and end apart: 10 -> 10, of which waited for: 3 -> 3; matrix products, arithmetic and copies ran while one was open for 0% -> 0% of each run, Pallas kernels for 20% -> 16%
where the time goes in v1:
time: 37.1 us
  Pallas kernels  20.1 us (54%)
  starting transfers between devices  14 us (38%)
  waiting for transfers between devices  2.21 us (6%)
  between operations  0.78 us (2%)
    pallas_call x1, Pallas kernels, run_models(): pl.pallas_call(functools.partial(model_kernel, workers, slots, levels, wi...  11.9 us
    ppermute x1, starting transfers between devices, body(): edge = lax.ppermute(edge, ('grp', 'crm'), pairs)  7.25 us
    ppermute x9, starting transfers between devices, exchange(): lax.ppermute(blocks[distance], axis, [(i, i ^ distance) for i in range(si...  6.78 us
    pallas_call x1, Pallas kernels, state_rows(): pl.pallas_call(functools.partial(state_kernel, slots, levels, width, colu...  2.67 us
    ppermute x9, waiting for transfers between devices, exchange(): lax.ppermute(blocks[distance], axis, [(i, i ^ distance) for i in range(si...  2.2 us
    pallas_call x1, Pallas kernels, body(): pl.pallas_call(functools.partial(gather_kernel, columns, capacity, worker...  1.66 us
    pallas_call x1, Pallas kernels, condensate(): pl.pallas_call(functools.partial(cloud_kernel, levels, width, workers, ca...  1.2 us
    pallas_call x1, Pallas kernels, pack(): pl.pallas_call(functools.partial(pack_kernel, capacity, workers), out_sha...  1.15 us
  transfers between devices with their start and end apart: 10, of which 3 were waited for; matrix products, arithmetic and copies ran while one was open for 0% of the time, Pallas kernels for 16%

profile of v1, /device:TPU:5, one launch (start us, length us, event | category | flops | bytes accessed | tf_op | source)
XLA Modules:
  0.0 37.1 jit_solution(4251807242374635757)
XLA Ops:
  0.6 1.1 %pack_forcing.1.refs_0_ = f32[24,128]{1,0:T(8,128)S(1)} custom-call(s32[24]{0:T(128)} %refs_0_.1, s32[24]{0:T(128)} %cost_hbm.1, f32[24,2,72]{2,1,0:T(2,128)} %forcing_hbm.1, f32[58,72]{1,0:T(8,128)} %refs_6_.1), custom_call_target="tpu_custom_call" | custom-call | tf_op jit(solution)/shard_map/pack_forcing/pallas_call | solution.py:96
  1.8 0.7 %collective-permute-start = (f32[24,128]{1,0:T(8,128)S(1)}, f32[24,128]{1,0:T(8,128)S(1)}, u32[]{:S(2)}, u32[]{:S(2)}) collective-permute-start(f32[24,128]{1,0:T(8,128)S(1)} %pack_forcing.1.refs_0_), channel_id=1, source_target_pairs={{0,1},{1,0},{2,3},{3,2},{4,5},{5,4},{6,7},{7,6},{8,9},{9,8},{10,11... | collective-permute-start | bytes 36872 | tf_op jit(solution)/shard_map/ppermute | solution.py:603
  2.5 0.0 collective-permute-start.1
  2.5 1.7 %collective-permute-start.2 = (f32[24,128]{1,0:T(8,128)S(1)}, f32[24,128]{1,0:T(8,128)S(1)}, u32[]{:S(2)}, u32[]{:S(2)}) collective-permute-start(f32[24,128]{1,0:T(8,128)S(1)} %pack_forcing.1.refs_0_), channel_id=1, source_target_pairs={{0,3},{1,2},{2,1},{3,0},{4,7},{5,6},{6,5},{7,4},{8,11},{9,10},{10,... | collective-permute-start | bytes 36872 | tf_op jit(solution)/shard_map/ppermute | solution.py:603
  4.2 0.0 collective-permute-done.refs_1_
  4.2 0.8 %collective-permute-done.1.refs_2_ = f32[24,128]{1,0:T(8,128)S(1)} collective-permute-done((f32[24,128]{1,0:T(8,128)S(1)}, f32[24,128]{1,0:T(8,128)S(1)}, u32[]{:S(2)}, u32[]{:S(2)}) %collective-permute-start.1) | collective-permute-done | bytes 12320 | tf_op jit(solution)/shard_map/ppermute | solution.py:603
  5.1 0.8 %collective-permute-done.2.refs_3_ = f32[24,128]{1,0:T(8,128)S(1)} collective-permute-done((f32[24,128]{1,0:T(8,128)S(1)}, f32[24,128]{1,0:T(8,128)S(1)}, u32[]{:S(2)}, u32[]{:S(2)}) %collective-permute-start.2) | collective-permute-done | bytes 12320 | tf_op jit(solution)/shard_map/ppermute | solution.py:603
  5.9 0.0 copy-start
  5.9 0.0 copy-start.1
  5.9 0.0 copy-start.2
  5.9 11.9 %cloud_models.1 = (f32[5,96,8,128]{3,2,1,0:T(8,128)S(1)}, f32[3,40,3712]{2,1,0:T(8,128)S(1)}, f32[40,128]{1,0:T(8,128)S(1)}, s32[8,128]{1,0:T(8,128)S(1)}) custom-call(f32[24,128]{1,0:T(8,128)S(1)} %pack_forcing.1.refs_0_, f32[24,128]{1,0:T(8,128)S(1)} %collective-permute-done.refs_1_, f32[24,128]{1,0:T(8,128)S(1)} %collective-permute-done.1.refs_2_, ...), custom_call_target="tpu_custom_call" | custom-call | bytes 41943040 | tf_op jit(solution)/shard_map/cloud_models/pallas_call | solution.py:450
  17.9 0.1 collective-permute-start.3
  17.9 0.1 collective-permute-start.4
  18.0 2.0 %collective-permute-start.5 = (f32[40,128]{1,0:T(8,128)S(1)}, f32[40,128]{1,0:T(8,128)S(1)}, u32[]{:S(2)}, u32[]{:S(2)}) collective-permute-start(f32[40,128]{1,0:T(8,128)S(1)} %get-tuple-element.46.t_ref.refs_0_), channel_id=1, source_target_pairs={{0,3},{1,2},{2,1},{3,0},{4,7},{5,6},{6,5},{7,4},{8,11},{9,10},{10,... | collective-permute-start | bytes 61448 | tf_op jit(solution)/shard_map/ppermute | solution.py:603
  20.1 1.2 %condensate.1 = (f32[40,3712]{1,0:T(8,128)S(1)}, f32[288,128]{1,0:T(8,128)S(1)}, f32[288,128]{1,0:T(8,128)S(1)}, f32[288,128]{1,0:T(8,128)S(1)}, f32[288,128]{1,0:T(8,128)S(1)}) custom-call(s32[8,128]{1,0:T(8,128)S(1)} %get-tuple-element.43.meta, f32[5,96,8,128]{3,2,1,0:T(8,128)S(1)} %get-tuple-element.34.fin, f32[40,128]{1,0:T(8,128)S(1)} %get-tuple-element.46.t_ref.refs_0_), custom_call_target="tpu_custom_call" | custom-call | bytes 8388608 | tf_op jit(solution)/shard_map/condensate/pallas_call | solution.py:481
  21.3 0.0 collective-permute-done.3.refs_1_
  21.3 0.0 collective-permute-done.4.refs_2_
  21.3 0.5 %collective-permute-done.5.refs_3_ = f32[40,128]{1,0:T(8,128)S(1)} collective-permute-done((f32[40,128]{1,0:T(8,128)S(1)}, f32[40,128]{1,0:T(8,128)S(1)}, u32[]{:S(2)}, u32[]{:S(2)}) %collective-permute-start.5) | collective-permute-done | bytes 20512 | tf_op jit(solution)/shard_map/ppermute | solution.py:603
  21.8 0.4 %collective-permute-start.6 = (f32[288,128]{1,0:T(8,128)S(1)}, f32[288,128]{1,0:T(8,128)S(1)}, u32[]{:S(2)}, u32[]{:S(2)}) collective-permute-start(f32[288,128]{1,0:T(8,128)S(1)} %get-tuple-element.54), channel_id=1, source_target_pairs={{0,1},{1,0},{2,3},{3,2},{4,5},{5,4},{6,7},{7,6},{8,9},{9,8},{10,11... | collective-permute-start | bytes 442376 | tf_op jit(solution)/shard_map/ppermute | solution.py:603
  22.2 1.4 %collective-permute-start.7 = (f32[288,128]{1,0:T(8,128)S(1)}, f32[288,128]{1,0:T(8,128)S(1)}, u32[]{:S(2)}, u32[]{:S(2)}) collective-permute-start(f32[288,128]{1,0:T(8,128)S(1)} %get-tuple-element.55), channel_id=1, source_target_pairs={{0,2},{1,3},{2,0},{3,1},{4,6},{5,7},{6,4},{7,5},{8,10},{9,11},{10,... | collective-permute-start | bytes 442376 | tf_op jit(solution)/shard_map/ppermute | solution.py:603
  23.6 0.4 collective-permute-start.8
  24.0 0.4 %edge_columns.1 = f32[24,128]{1,0:T(8,128)S(1)} custom-call(f32[40,128]{1,0:T(8,128)S(1)} %get-tuple-element.46.t_ref.refs_0_, f32[40,128]{1,0:T(8,128)S(1)} %collective-permute-done.3.refs_1_, f32[40,128]{1,0:T(8,128)S(1)} %collective-permute-done.4.refs_2_, f32[40,128]{1,0:T(8,128)S(1)} %collective-permute-done.5.refs_3_), custom_call_target="tpu_custom_call" | custom-call | bytes 1048576 | tf_op jit(solution)/shard_map/edge_columns/pallas_call | solution.py:624
  24.4 7.3 %collective-permute-start.9 = (f32[24,128]{1,0:T(8,128)S(1)}, f32[24,128]{1,0:T(8,128)S(1)}, u32[]{:S(2)}, u32[]{:S(2)}) collective-permute-start(f32[24,128]{1,0:T(8,128)S(1)} %edge_columns.1), channel_id=1, source_target_pairs={{0,4},{7,3},{4,8},{11,7},{8,12},{15,11},{12,16},{19,15},{16,20},{2... | collective-permute-start | bytes 36872 | tf_op jit(solution)/shard_map/ppermute | solution.py:637
  31.6 0.0 copy-done
  31.6 0.0 copy-done.1
  31.7 0.0 copy-done.2
  31.7 0.0 copy-start.3
  31.7 2.7 %state_rows.1 = (f32[3,36,3712]{2,1,0:T(8,128)}, f32[24,128]{1,0:T(8,128)S(1)}, f32[2,128,72]{2,1,0:T(8,128)S(1)}) custom-call(s32[8,128]{1,0:T(8,128)S(1)} %get-tuple-element.43.meta, f32[5,96,8,128]{3,2,1,0:T(8,128)S(1)} %get-tuple-element.34.fin, f32[40,128]{1,0:T(8,128)S(1)} %get-tuple-element.46.t_ref.refs_0_, f32[40,3712]{1,0:T(8,128)S(1)} %get-tuple-element.44.water, ...), custom_call_target="tpu_custom_call" | custom-call | bytes 12582912 | tf_op jit(solution)/shard_map/state_rows/pallas_call | solution.py:498
  34.4 0.0 collective-permute-done.6.refs_2_
  34.4 0.0 collective-permute-done.7.refs_3_
  34.4 0.0 collective-permute-done.8.refs_4_
  34.4 0.0 copy-done.3
  34.4 1.7 %cloud_rows.1 = f32[24,3712]{1,0:T(8,128)} custom-call(s32[24]{0:T(128)S(1)} %copy-done.3, f32[288,128]{1,0:T(8,128)S(1)} %get-tuple-element.53.refs_1_, f32[288,128]{1,0:T(8,128)S(1)} %collective-permute-done.6.refs_2_, f32[288,128]{1,0:T(8,128)S(1)} %collective-permute-done.7.refs_3_, f32[288,128]{1,0:T(8,128)S(1)} %collective-permute-done.8.refs_4_), custom_call_target="tpu_custom_call" | custom-call | bytes 1048576 | tf_op jit(solution)/shard_map/cloud_rows/pallas_call | solution.py:642
  36.1 0.0 collective-permute-done.9.edge
  36.1 1.1 %physics_cells.1 = f32[24,2,72]{2,1,0:T(2,128)} custom-call(f32[24,128]{1,0:T(8,128)S(1)} %get-tuple-element.58.inner, f32[2,128,72]{2,1,0:T(8,128)S(1)} %get-tuple-element.59.maps, f32[24,128]{1,0:T(8,128)S(1)} %collective-permute-done.9.edge, s32[4,24]{1,0:T(4,128)S(1)} %bitcast.5, f32[4,24]{1,0:T(4,128)S(1)} %bitcast.7), custom_call_target="tpu_custom_call" | custom-call | bytes 1048576 | tf_op jit(solution)/shard_map/physics_cells/pallas_call | solution.py:655
Async XLA Ops:
  1.8 2.5 %collective-permute-start = (f32[24,128]{1,0:T(8,128)S(1)}, f32[24,128]{1,0:T(8,128)S(1)}, u32[]{:S(2)}, u32[]{:S(2)}) collective-permute-start(f32[24,128]{1,0:T(8,128)S(1)} %pack_forcing.1.refs_0_), channel_id=1, source_target_pairs={{0,1},{1,0},{2,3},{3,2},{4,5},{5,4},{6,7},{7,6},{8,9},{9,8},{10,11... | collective-permute-start | bytes 36872 | tf_op jit(solution)/shard_map/ppermute | solution.py:603
  2.5 2.6 %collective-permute-start.1 = (f32[24,128]{1,0:T(8,128)S(1)}, f32[24,128]{1,0:T(8,128)S(1)}, u32[]{:S(2)}, u32[]{:S(2)}) collective-permute-start(f32[24,128]{1,0:T(8,128)S(1)} %pack_forcing.1.refs_0_), channel_id=1, source_target_pairs={{0,2},{1,3},{2,0},{3,1},{4,6},{5,7},{6,4},{7,5},{8,10},{9,11},{10,... | collective-permute-start | bytes 36872 | tf_op jit(solution)/shard_map/ppermute | solution.py:603
  2.5 3.4 %collective-permute-start.2 = (f32[24,128]{1,0:T(8,128)S(1)}, f32[24,128]{1,0:T(8,128)S(1)}, u32[]{:S(2)}, u32[]{:S(2)}) collective-permute-start(f32[24,128]{1,0:T(8,128)S(1)} %pack_forcing.1.refs_0_), channel_id=1, source_target_pairs={{0,3},{1,2},{2,1},{3,0},{4,7},{5,6},{6,5},{7,4},{8,11},{9,10},{10,... | collective-permute-start | bytes 36872 | tf_op jit(solution)/shard_map/ppermute | solution.py:603
  5.9 25.7 %copy-start = (f32[58,72]{1,0:T(8,128)S(1)}, f32[58,72]{1,0:T(8,128)}, u32[]{:S(2)}) copy-start(f32[58,72]{1,0:T(8,128)} %refs_6_.1) | copy-start | bytes 50116
  5.9 25.7 %copy-start.1 = (s32[24,4]{0,1:T(4,128)S(1)}, s32[24,4]{0,1:T(4,128)}, u32[]{:S(2)}) copy-start(s32[24,4]{0,1:T(4,128)} %param.12) | copy-start | bytes 1156
  5.9 25.7 %copy-start.2 = (f32[24,4]{0,1:T(4,128)S(1)}, f32[24,4]{0,1:T(4,128)}, u32[]{:S(2)}) copy-start(f32[24,4]{0,1:T(4,128)} %param.13) | copy-start | bytes 1156
  17.9 3.4 %collective-permute-start.3 = (f32[40,128]{1,0:T(8,128)S(1)}, f32[40,128]{1,0:T(8,128)S(1)}, u32[]{:S(2)}, u32[]{:S(2)}) collective-permute-start(f32[40,128]{1,0:T(8,128)S(1)} %get-tuple-element.46.t_ref.refs_0_), channel_id=1, source_target_pairs={{0,1},{1,0},{2,3},{3,2},{4,5},{5,4},{6,7},{7,6},{8,9},{9,8},{10,11... | collective-permute-start | bytes 61448 | tf_op jit(solution)/shard_map/ppermute | solution.py:603
  17.9 3.4 %collective-permute-start.4 = (f32[40,128]{1,0:T(8,128)S(1)}, f32[40,128]{1,0:T(8,128)S(1)}, u32[]{:S(2)}, u32[]{:S(2)}) collective-permute-start(f32[40,128]{1,0:T(8,128)S(1)} %get-tuple-element.46.t_ref.refs_0_), channel_id=1, source_target_pairs={{0,2},{1,3},{2,0},{3,1},{4,6},{5,7},{6,4},{7,5},{8,10},{9,11},{10,... | collective-permute-start | bytes 61448 | tf_op jit(solution)/shard_map/ppermute | solution.py:603
  18.0 3.8 %collective-permute-start.5 = (f32[40,128]{1,0:T(8,128)S(1)}, f32[40,128]{1,0:T(8,128)S(1)}, u32[]{:S(2)}, u32[]{:S(2)}) collective-permute-start(f32[40,128]{1,0:T(8,128)S(1)} %get-tuple-element.46.t_ref.refs_0_), channel_id=1, source_target_pairs={{0,3},{1,2},{2,1},{3,0},{4,7},{5,6},{6,5},{7,4},{8,11},{9,10},{10,... | collective-permute-start | bytes 61448 | tf_op jit(solution)/shard_map/ppermute | solution.py:603
  21.8 12.5 %collective-permute-start.6 = (f32[288,128]{1,0:T(8,128)S(1)}, f32[288,128]{1,0:T(8,128)S(1)}, u32[]{:S(2)}, u32[]{:S(2)}) collective-permute-start(f32[288,128]{1,0:T(8,128)S(1)} %get-tuple-element.54), channel_id=1, source_target_pairs={{0,1},{1,0},{2,3},{3,2},{4,5},{5,4},{6,7},{7,6},{8,9},{9,8},{10,11... | collective-permute-start | bytes 442376 | tf_op jit(solution)/shard_map/ppermute | solution.py:603
  22.2 12.2 %collective-permute-start.7 = (f32[288,128]{1,0:T(8,128)S(1)}, f32[288,128]{1,0:T(8,128)S(1)}, u32[]{:S(2)}, u32[]{:S(2)}) collective-permute-start(f32[288,128]{1,0:T(8,128)S(1)} %get-tuple-element.55), channel_id=1, source_target_pairs={{0,2},{1,3},{2,0},{3,1},{4,6},{5,7},{6,4},{7,5},{8,10},{9,11},{10,... | collective-permute-start | bytes 442376 | tf_op jit(solution)/shard_map/ppermute | solution.py:603
  23.6 10.8 %collective-permute-start.8 = (f32[288,128]{1,0:T(8,128)S(1)}, f32[288,128]{1,0:T(8,128)S(1)}, u32[]{:S(2)}, u32[]{:S(2)}) collective-permute-start(f32[288,128]{1,0:T(8,128)S(1)} %get-tuple-element.56), channel_id=1, source_target_pairs={{0,3},{1,2},{2,1},{3,0},{4,7},{5,6},{6,5},{7,4},{8,11},{9,10},{10,... | collective-permute-start | bytes 442376 | tf_op jit(solution)/shard_map/ppermute | solution.py:603
  24.4 11.7 %collective-permute-start.9 = (f32[24,128]{1,0:T(8,128)S(1)}, f32[24,128]{1,0:T(8,128)S(1)}, u32[]{:S(2)}, u32[]{:S(2)}) collective-permute-start(f32[24,128]{1,0:T(8,128)S(1)} %edge_columns.1), channel_id=1, source_target_pairs={{0,4},{7,3},{4,8},{11,7},{8,12},{15,11},{12,16},{19,15},{16,20},{2... | collective-permute-start | bytes 36872 | tf_op jit(solution)/shard_map/ppermute | solution.py:637
  31.7 2.7 %copy-start.3 = (s32[24]{0:T(128)S(1)}, s32[24]{0:T(128)}, u32[]{:S(2)}) copy-start(s32[24]{0:T(128)} %refs_0_.1) | copy-start | bytes 292

commit v2 on v1

--- a/solution.py
+++ b/solution.py
@@ -555,25 +555,11 @@
         maps[variable] = dot_t(place, level_map[...])
 
 
-def physics_kernel(columns, workers, inner, maps, edge, index, weight, out):
-    me = lax.axis_index("crm")
-    edge_sub = iota((columns, 1), 0)
-    edge_block = jnp.where(me == 0, 0, jnp.where(me == workers - 1, 2, -3))
-    ident = (edge_block * columns + edge_sub).astype(F32)
-    wanted, share = share_rows(index, weight)
-    mix = jnp.zeros((columns, columns), F32)
-    for source in range(index.shape[0]):
-        mix = mix + jnp.where(ident == wanted[source : source + 1], share[source : source + 1], 0.0)
-    mixed = inner[...] + dot_t(mix, jnp.where(edge_block >= 0, edge[...], 0.0))
-    for variable in range(2):
-        out[:, variable, :] = dot(mixed, maps[variable])
-
-
-def gather_kernel(columns, capacity, workers, *refs):
+def finish_kernel(columns, capacity, workers, *refs):
     target = refs[0]
     received = refs[1 : workers + 1]
-    out, counts, column_of, places = refs[workers + 1 :]
-    tiles = out.shape[1] // LANES
+    inner, maps, edge, index, weight, cloud_hbm, physics_hbm, counts, column_of, places, cloud, physics, sems = refs[workers + 1 :]
+    tiles = cloud.shape[1] // LANES
     block = -(-tiles // ROWS) * ROWS
     me = lax.axis_index("crm")
     for worker in range(workers):
@@ -589,11 +575,31 @@
         for rank in range(capacity):
             place = pl.multiple_of(column_of[distance * capacity + rank] * block, ROWS)
             places[pl.ds(place, block), :] = received[distance][rank * block : (rank + 1) * block, :]
-    for base in range(0, columns, ROWS):
-        count = min(ROWS, columns - base)
+    chunk = ROWS if columns % ROWS == 0 else columns
+    copies = []
+    for base in range(0, columns, chunk):
         for tile in range(tiles):
-            rows = places[pl.ds(base * block + tile, count, stride=block), :]
-            out[base : base + count, tile * LANES : (tile + 1) * LANES] = rows
+            rows = places[pl.ds(base * block + tile, chunk, stride=block), :]
+            cloud[base : base + chunk, tile * LANES : (tile + 1) * LANES] = rows
+        copies.append(
+            pltpu.make_async_copy(cloud.at[pl.ds(base, chunk), :], cloud_hbm.at[pl.ds(base, chunk), :], sems.at[len(copies)])
+        )
+        copies[-1].start()
+
+    edge_sub = iota((columns, 1), 0)
+    edge_block = jnp.where(me == 0, 0, jnp.where(me == workers - 1, 2, -3))
+    ident = (edge_block * columns + edge_sub).astype(F32)
+    wanted, share = share_rows(index, weight)
+    mix = jnp.zeros((columns, columns), F32)
+    for source in range(index.shape[0]):
+        mix = mix + jnp.where(ident == wanted[source : source + 1], share[source : source + 1], 0.0)
+    mixed = inner[...] + dot_t(mix, jnp.where(edge_block >= 0, edge[...], 0.0))
+    for variable in range(2):
+        physics[:, variable, :] = dot(mixed, maps[variable])
+    copies.append(pltpu.make_async_copy(physics, physics_hbm, sems.at[len(copies)]))
+    copies[-1].start()
+    for copy in copies:
+        copy.wait()
 
 
 def exchange(blocks, axis):
@@ -631,34 +637,30 @@
     pairs = []
     for group in range(groups):
         after = (group + 1) % groups
-        pairs.append((group * workers, after * workers))
-        pairs.append((after * workers + workers - 1, group * workers + workers - 1))
+        for worker in range(workers):
+            ends = (group * workers + worker, after * workers + worker)
+            pairs.append(ends if 2 * worker < workers else ends[::-1])
     edge, meta, tendencies = lax.optimization_barrier((edge, meta, tendencies))
     edge = lax.ppermute(edge, ("grp", "crm"), pairs)
     state, inner, maps = state_rows(
         slots, levels, columns, meta, fin, tendency, water, start, tendencies, remap_index.T, remap_weight.T, level_map
     )
     block = clouds[0].shape[0] // capacity
-    cloud_water = pl.pallas_call(
-        functools.partial(gather_kernel, columns, capacity, workers),
-        out_shape=jax.ShapeDtypeStruct((columns, cells), F32),
-        in_specs=[pl.BlockSpec(memory_space=pltpu.SMEM)] + [vmem] * workers,
-        out_specs=vmem,
+    cloud_water, physics = pl.pallas_call(
+        functools.partial(finish_kernel, columns, capacity, workers),
+        out_shape=[jax.ShapeDtypeStruct((columns, cells), F32), jax.ShapeDtypeStruct((columns, 2, gcm), F32)],
+        in_specs=[pl.BlockSpec(memory_space=pltpu.SMEM)] + [vmem] * (workers + 5),
+        out_specs=[pl.BlockSpec(memory_space=pl.ANY)] * 2,
         scratch_shapes=[
             pltpu.SMEM((workers,), jnp.int32),
             pltpu.SMEM((slots,), jnp.int32),
             pltpu.VMEM(((columns + 1) * block, LANES), F32),
+            pltpu.VMEM((columns, cells), F32),
+            pltpu.VMEM((columns, 2, gcm), F32),
+            pltpu.SemaphoreType.DMA((-(-columns // ROWS) + 1,)),
         ],
-        **small("cloud_rows"),
-    )(target, *clouds)
-    inner, maps, cloud_water = lax.optimization_barrier((inner, maps, cloud_water))
-    physics = pl.pallas_call(
-        functools.partial(physics_kernel, columns, workers),
-        out_shape=jax.ShapeDtypeStruct((columns, 2, gcm), F32),
-        in_specs=[vmem] * 5,
-        out_specs=vmem,
-        **small("physics_cells"),
-    )(inner, maps, edge, remap_index.T, remap_weight.T)
+        **small("columns_out"),
+    )(target, *clouds, inner, maps, edge, remap_index.T, remap_weight.T)
     return state.transpose(1, 0, 2), cloud_water, physics
 
 

time: 37.1 us -> 34.7 us (0.935)
  the two profiles are of different devices: /device:TPU:5 before, /device:TPU:0 now
where the time goes in v2:
time: 34.7 us
  Pallas kernels  19.2 us (55%)
  starting transfers between devices  7.57 us (22%)
  waiting for transfers between devices  7.23 us (21%)
  between operations  0.71 us (2%)
    pallas_call x1, Pallas kernels, run_models(): pl.pallas_call(functools.partial(model_kernel, workers, slots, levels, wi...  11.9 us
    ppermute x9, starting transfers between devices, exchange(): lax.ppermute(blocks[distance], axis, [(i, i ^ distance) for i in range(si...  6.92 us
    ppermute x9, waiting for transfers between devices, exchange(): lax.ppermute(blocks[distance], axis, [(i, i ^ distance) for i in range(si...  4.12 us
    ppermute x1, waiting for transfers between devices, body(): edge = lax.ppermute(edge, ('grp', 'crm'), pairs)  3.11 us
    pallas_call x1, Pallas kernels, state_rows(): pl.pallas_call(functools.partial(state_kernel, slots, levels, width, colu...  2.67 us
    pallas_call x1, Pallas kernels, body(): pl.pallas_call(functools.partial(finish_kernel, columns, capacity, worker...  1.84 us
    pallas_call x1, Pallas kernels, condensate(): pl.pallas_call(functools.partial(cloud_kernel, levels, width, workers, ca...  1.2 us
    pallas_call x1, Pallas kernels, pack(): pl.pallas_call(functools.partial(pack_kernel, capacity, workers), out_sha...  1.15 us
  transfers between devices with their start and end apart: 10, of which 6 were waited for; matrix products, arithmetic and copies ran while one was open for 0% of the time, Pallas kernels for 12%

profile of v2, /device:TPU:0, one launch (start us, length us, event | category | flops | bytes accessed | tf_op | source)
XLA Modules:
  0.0 34.7 jit_solution(6731148187227555263)
XLA Ops:
  0.6 1.1 %pack_forcing.1.refs_0_ = f32[24,128]{1,0:T(8,128)S(1)} custom-call(s32[24]{0:T(128)} %refs_0_.1, s32[24]{0:T(128)} %cost_hbm.1, f32[24,2,72]{2,1,0:T(2,128)} %forcing_hbm.1, f32[58,72]{1,0:T(8,128)} %refs_6_.1), custom_call_target="tpu_custom_call" | custom-call | tf_op jit(solution)/shard_map/pack_forcing/pallas_call | solution.py:96
  1.8 2.5 %collective-permute-start.2 = (f32[24,128]{1,0:T(8,128)S(1)}, f32[24,128]{1,0:T(8,128)S(1)}, u32[]{:S(2)}, u32[]{:S(2)}) collective-permute-start(f32[24,128]{1,0:T(8,128)S(1)} %pack_forcing.1.refs_0_), channel_id=1, source_target_pairs={{0,3},{1,2},{2,1},{3,0},{4,7},{5,6},{6,5},{7,4},{8,11},{9,10},{10,... | collective-permute-start | bytes 36872 | tf_op jit(solution)/shard_map/ppermute | solution.py:609
  4.3 0.6 %collective-permute-start.1 = (f32[24,128]{1,0:T(8,128)S(1)}, f32[24,128]{1,0:T(8,128)S(1)}, u32[]{:S(2)}, u32[]{:S(2)}) collective-permute-start(f32[24,128]{1,0:T(8,128)S(1)} %pack_forcing.1.refs_0_), channel_id=1, source_target_pairs={{0,2},{1,3},{2,0},{3,1},{4,6},{5,7},{6,4},{7,5},{8,10},{9,11},{10,... | collective-permute-start | bytes 36872 | tf_op jit(solution)/shard_map/ppermute | solution.py:609
  4.9 0.0 collective-permute-start
  4.9 0.7 %collective-permute-done.2.refs_3_ = f32[24,128]{1,0:T(8,128)S(1)} collective-permute-done((f32[24,128]{1,0:T(8,128)S(1)}, f32[24,128]{1,0:T(8,128)S(1)}, u32[]{:S(2)}, u32[]{:S(2)}) %collective-permute-start.2) | collective-permute-done | bytes 12320 | tf_op jit(solution)/shard_map/ppermute | solution.py:609
  5.7 2.3 %collective-permute-done.1.refs_2_ = f32[24,128]{1,0:T(8,128)S(1)} collective-permute-done((f32[24,128]{1,0:T(8,128)S(1)}, f32[24,128]{1,0:T(8,128)S(1)}, u32[]{:S(2)}, u32[]{:S(2)}) %collective-permute-start.1) | collective-permute-done | bytes 12320 | tf_op jit(solution)/shard_map/ppermute | solution.py:609
  8.0 0.0 collective-permute-done.refs_1_
  8.0 0.0 copy-start
  8.0 0.0 copy-start.1
  8.0 0.0 copy-start.2
  8.0 11.9 %cloud_models.1 = (f32[5,96,8,128]{3,2,1,0:T(8,128)S(1)}, f32[3,40,3712]{2,1,0:T(8,128)S(1)}, f32[40,128]{1,0:T(8,128)S(1)}, s32[8,128]{1,0:T(8,128)S(1)}) custom-call(f32[24,128]{1,0:T(8,128)S(1)} %pack_forcing.1.refs_0_, f32[24,128]{1,0:T(8,128)S(1)} %collective-permute-done.refs_1_, f32[24,128]{1,0:T(8,128)S(1)} %collective-permute-done.1.refs_2_, ...), custom_call_target="tpu_custom_call" | custom-call | bytes 41943040 | tf_op jit(solution)/shard_map/cloud_models/pallas_call | solution.py:450
  19.9 0.1 collective-permute-start.5
  20.0 0.1 collective-permute-start.4
  20.1 1.8 %collective-permute-start.3 = (f32[40,128]{1,0:T(8,128)S(1)}, f32[40,128]{1,0:T(8,128)S(1)}, u32[]{:S(2)}, u32[]{:S(2)}) collective-permute-start(f32[40,128]{1,0:T(8,128)S(1)} %get-tuple-element.45.t_ref.refs_0_), channel_id=1, source_target_pairs={{0,1},{1,0},{2,3},{3,2},{4,5},{5,4},{6,7},{7,6},{8,9},{9,8},{10,11... | collective-permute-start | bytes 61448 | tf_op jit(solution)/shard_map/ppermute | solution.py:609
  21.8 1.2 %condensate.1 = (f32[40,3712]{1,0:T(8,128)S(1)}, f32[288,128]{1,0:T(8,128)S(1)}, f32[288,128]{1,0:T(8,128)S(1)}, f32[288,128]{1,0:T(8,128)S(1)}, f32[288,128]{1,0:T(8,128)S(1)}) custom-call(s32[8,128]{1,0:T(8,128)S(1)} %get-tuple-element.42.meta, f32[5,96,8,128]{3,2,1,0:T(8,128)S(1)} %get-tuple-element.33.fin, f32[40,128]{1,0:T(8,128)S(1)} %get-tuple-element.45.t_ref.refs_0_), custom_call_target="tpu_custom_call" | custom-call | bytes 8388608 | tf_op jit(solution)/shard_map/condensate/pallas_call | solution.py:481
  23.0 0.1 collective-permute-done.5.refs_3_
  23.2 0.7 %collective-permute-done.4.refs_2_ = f32[40,128]{1,0:T(8,128)S(1)} collective-permute-done((f32[40,128]{1,0:T(8,128)S(1)}, f32[40,128]{1,0:T(8,128)S(1)}, u32[]{:S(2)}, u32[]{:S(2)}) %collective-permute-start.4) | collective-permute-done | bytes 20512 | tf_op jit(solution)/shard_map/ppermute | solution.py:609
  23.8 0.0 collective-permute-done.3.refs_1_
  23.8 0.0 collective-permute-start.6
  23.8 0.9 %collective-permute-start.7 = (f32[288,128]{1,0:T(8,128)S(1)}, f32[288,128]{1,0:T(8,128)S(1)}, u32[]{:S(2)}, u32[]{:S(2)}) collective-permute-start(f32[288,128]{1,0:T(8,128)S(1)} %get-tuple-element.52), channel_id=1, source_target_pairs={{0,2},{1,3},{2,0},{3,1},{4,6},{5,7},{6,4},{7,5},{8,10},{9,11},{10,... | collective-permute-start | bytes 442376 | tf_op jit(solution)/shard_map/ppermute | solution.py:609
  24.8 0.9 %collective-permute-start.8 = (f32[288,128]{1,0:T(8,128)S(1)}, f32[288,128]{1,0:T(8,128)S(1)}, u32[]{:S(2)}, u32[]{:S(2)}) collective-permute-start(f32[288,128]{1,0:T(8,128)S(1)} %get-tuple-element.53), channel_id=1, source_target_pairs={{0,3},{1,2},{2,1},{3,0},{4,7},{5,6},{6,5},{7,4},{8,11},{9,10},{10,... | collective-permute-start | bytes 442376 | tf_op jit(solution)/shard_map/ppermute | solution.py:609
  25.7 0.4 %edge_columns.1 = f32[24,128]{1,0:T(8,128)S(1)} custom-call(f32[40,128]{1,0:T(8,128)S(1)} %get-tuple-element.45.t_ref.refs_0_, f32[40,128]{1,0:T(8,128)S(1)} %collective-permute-done.3.refs_1_, f32[40,128]{1,0:T(8,128)S(1)} %collective-permute-done.4.refs_2_, f32[40,128]{1,0:T(8,128)S(1)} %collective-permute-done.5.refs_3_), custom_call_target="tpu_custom_call" | custom-call | bytes 1048576 | tf_op jit(solution)/shard_map/edge_columns/pallas_call | solution.py:630
  26.1 0.6 %collective-permute-start.9 = (f32[24,128]{1,0:T(8,128)S(1)}, f32[24,128]{1,0:T(8,128)S(1)}, u32[]{:S(2)}, u32[]{:S(2)}) collective-permute-start(f32[24,128]{1,0:T(8,128)S(1)} %edge_columns.1), channel_id=1, source_target_pairs={{0,4},{1,5},{6,2},{7,3},{4,8},{5,9},{10,6},{11,7},{8,12},{9,13},{1... | collective-permute-start | bytes 36872 | tf_op jit(solution)/shard_map/ppermute | solution.py:644
  26.8 0.0 copy-done
  26.8 0.0 copy-done.1
  26.8 0.0 copy-done.2
  26.8 0.0 copy-start.3
  26.8 2.7 %state_rows.1 = (f32[3,36,3712]{2,1,0:T(8,128)}, f32[24,128]{1,0:T(8,128)S(1)}, f32[2,128,72]{2,1,0:T(8,128)S(1)}) custom-call(s32[8,128]{1,0:T(8,128)S(1)} %get-tuple-element.42.meta, f32[5,96,8,128]{3,2,1,0:T(8,128)S(1)} %get-tuple-element.33.fin, f32[40,128]{1,0:T(8,128)S(1)} %get-tuple-element.45.t_ref.refs_0_, f32[40,3712]{1,0:T(8,128)S(1)} %get-tuple-element.43.water, ...), custom_call_target="tpu_custom_call" | custom-call | bytes 12582912 | tf_op jit(solution)/shard_map/state_rows/pallas_call | solution.py:498
  29.5 3.1 %collective-permute-done.9.refs_7_ = f32[24,128]{1,0:T(8,128)S(1)} collective-permute-done((f32[24,128]{1,0:T(8,128)S(1)}, f32[24,128]{1,0:T(8,128)S(1)}, u32[]{:S(2)}, u32[]{:S(2)}) %collective-permute-start.9) | collective-permute-done | bytes 12320 | tf_op jit(solution)/shard_map/ppermute | solution.py:644
  32.6 0.0 collective-permute-done.6.refs_2_
  32.6 0.0 collective-permute-done.7.refs_3_
  32.6 0.3 collective-permute-done.8.refs_4_
  32.9 0.0 copy-done.3
  32.9 1.8 %columns_out.1 = (f32[24,3712]{1,0:T(8,128)}, f32[24,2,72]{2,1,0:T(2,128)}) custom-call(s32[24]{0:T(128)S(1)} %copy-done.3, f32[288,128]{1,0:T(8,128)S(1)} %get-tuple-element.50.refs_1_, f32[288,128]{1,0:T(8,128)S(1)} %collective-permute-done.6.refs_2_, f32[288,128]{1,0:T(8,128)S(1)} %collective-permute-done.7.refs_3_, ...), custom_call_target="tpu_custom_call" | custom-call | bytes 1048576 | tf_op jit(solution)/shard_map/columns_out/pallas_call | solution.py:649
Async XLA Ops:
  1.8 3.9 %collective-permute-start.2 = (f32[24,128]{1,0:T(8,128)S(1)}, f32[24,128]{1,0:T(8,128)S(1)}, u32[]{:S(2)}, u32[]{:S(2)}) collective-permute-start(f32[24,128]{1,0:T(8,128)S(1)} %pack_forcing.1.refs_0_), channel_id=1, source_target_pairs={{0,3},{1,2},{2,1},{3,0},{4,7},{5,6},{6,5},{7,4},{8,11},{9,10},{10,... | collective-permute-start | bytes 36872 | tf_op jit(solution)/shard_map/ppermute | solution.py:609
  4.3 3.7 %collective-permute-start.1 = (f32[24,128]{1,0:T(8,128)S(1)}, f32[24,128]{1,0:T(8,128)S(1)}, u32[]{:S(2)}, u32[]{:S(2)}) collective-permute-start(f32[24,128]{1,0:T(8,128)S(1)} %pack_forcing.1.refs_0_), channel_id=1, source_target_pairs={{0,2},{1,3},{2,0},{3,1},{4,6},{5,7},{6,4},{7,5},{8,10},{9,11},{10,... | collective-permute-start | bytes 36872 | tf_op jit(solution)/shard_map/ppermute | solution.py:609
  4.9 3.1 %collective-permute-start = (f32[24,128]{1,0:T(8,128)S(1)}, f32[24,128]{1,0:T(8,128)S(1)}, u32[]{:S(2)}, u32[]{:S(2)}) collective-permute-start(f32[24,128]{1,0:T(8,128)S(1)} %pack_forcing.1.refs_0_), channel_id=1, source_target_pairs={{0,1},{1,0},{2,3},{3,2},{4,5},{5,4},{6,7},{7,6},{8,9},{9,8},{10,11... | collective-permute-start | bytes 36872 | tf_op jit(solution)/shard_map/ppermute | solution.py:609
  8.0 18.8 %copy-start = (f32[58,72]{1,0:T(8,128)S(1)}, f32[58,72]{1,0:T(8,128)}, u32[]{:S(2)}) copy-start(f32[58,72]{1,0:T(8,128)} %refs_6_.1) | copy-start | bytes 50116
  8.0 18.8 %copy-start.1 = (s32[24,4]{0,1:T(4,128)S(1)}, s32[24,4]{0,1:T(4,128)}, u32[]{:S(2)}) copy-start(s32[24,4]{0,1:T(4,128)} %param.12) | copy-start | bytes 1156
  8.0 18.8 %copy-start.2 = (f32[24,4]{0,1:T(4,128)S(1)}, f32[24,4]{0,1:T(4,128)}, u32[]{:S(2)}) copy-start(f32[24,4]{0,1:T(4,128)} %param.13) | copy-start | bytes 1156
  19.9 3.3 %collective-permute-start.5 = (f32[40,128]{1,0:T(8,128)S(1)}, f32[40,128]{1,0:T(8,128)S(1)}, u32[]{:S(2)}, u32[]{:S(2)}) collective-permute-start(f32[40,128]{1,0:T(8,128)S(1)} %get-tuple-element.45.t_ref.refs_0_), channel_id=1, source_target_pairs={{0,3},{1,2},{2,1},{3,0},{4,7},{5,6},{6,5},{7,4},{8,11},{9,10},{10,... | collective-permute-start | bytes 61448 | tf_op jit(solution)/shard_map/ppermute | solution.py:609
  20.0 3.8 %collective-permute-start.4 = (f32[40,128]{1,0:T(8,128)S(1)}, f32[40,128]{1,0:T(8,128)S(1)}, u32[]{:S(2)}, u32[]{:S(2)}) collective-permute-start(f32[40,128]{1,0:T(8,128)S(1)} %get-tuple-element.45.t_ref.refs_0_), channel_id=1, source_target_pairs={{0,2},{1,3},{2,0},{3,1},{4,6},{5,7},{6,4},{7,5},{8,10},{9,11},{10,... | collective-permute-start | bytes 61448 | tf_op jit(solution)/shard_map/ppermute | solution.py:609
  20.1 3.8 %collective-permute-start.3 = (f32[40,128]{1,0:T(8,128)S(1)}, f32[40,128]{1,0:T(8,128)S(1)}, u32[]{:S(2)}, u32[]{:S(2)}) collective-permute-start(f32[40,128]{1,0:T(8,128)S(1)} %get-tuple-element.45.t_ref.refs_0_), channel_id=1, source_target_pairs={{0,1},{1,0},{2,3},{3,2},{4,5},{5,4},{6,7},{7,6},{8,9},{9,8},{10,11... | collective-permute-start | bytes 61448 | tf_op jit(solution)/shard_map/ppermute | solution.py:609
  23.8 8.7 %collective-permute-start.6 = (f32[288,128]{1,0:T(8,128)S(1)}, f32[288,128]{1,0:T(8,128)S(1)}, u32[]{:S(2)}, u32[]{:S(2)}) collective-permute-start(f32[288,128]{1,0:T(8,128)S(1)} %get-tuple-element.51), channel_id=1, source_target_pairs={{0,1},{1,0},{2,3},{3,2},{4,5},{5,4},{6,7},{7,6},{8,9},{9,8},{10,11... | collective-permute-start | bytes 442376 | tf_op jit(solution)/shard_map/ppermute | solution.py:609
  23.8 8.7 %collective-permute-start.7 = (f32[288,128]{1,0:T(8,128)S(1)}, f32[288,128]{1,0:T(8,128)S(1)}, u32[]{:S(2)}, u32[]{:S(2)}) collective-permute-start(f32[288,128]{1,0:T(8,128)S(1)} %get-tuple-element.52), channel_id=1, source_target_pairs={{0,2},{1,3},{2,0},{3,1},{4,6},{5,7},{6,4},{7,5},{8,10},{9,11},{10,... | collective-permute-start | bytes 442376 | tf_op jit(solution)/shard_map/ppermute | solution.py:609
  24.8 8.1 %collective-permute-start.8 = (f32[288,128]{1,0:T(8,128)S(1)}, f32[288,128]{1,0:T(8,128)S(1)}, u32[]{:S(2)}, u32[]{:S(2)}) collective-permute-start(f32[288,128]{1,0:T(8,128)S(1)} %get-tuple-element.53), channel_id=1, source_target_pairs={{0,3},{1,2},{2,1},{3,0},{4,7},{5,6},{6,5},{7,4},{8,11},{9,10},{10,... | collective-permute-start | bytes 442376 | tf_op jit(solution)/shard_map/ppermute | solution.py:609
  26.1 6.4 %collective-permute-start.9 = (f32[24,128]{1,0:T(8,128)S(1)}, f32[24,128]{1,0:T(8,128)S(1)}, u32[]{:S(2)}, u32[]{:S(2)}) collective-permute-start(f32[24,128]{1,0:T(8,128)S(1)} %edge_columns.1), channel_id=1, source_target_pairs={{0,4},{1,5},{6,2},{7,3},{4,8},{5,9},{10,6},{11,7},{8,12},{9,13},{1... | collective-permute-start | bytes 36872 | tf_op jit(solution)/shard_map/ppermute | solution.py:644
  26.8 6.1 %copy-start.3 = (s32[24]{0:T(128)S(1)}, s32[24]{0:T(128)}, u32[]{:S(2)}) copy-start(s32[24]{0:T(128)} %refs_0_.1) | copy-start | bytes 292

commit v3 on v2

--- a/solution.py
+++ b/solution.py
@@ -152,12 +152,9 @@
     fetch.start()
     fetch.wait()
 
-    def load(index, carry):
+    for index in range(padded):
         slot = meta_s[0, index]
         pltpu.make_async_copy(x_hbm.at[:, pl.ds(slot, 1), :], xs.at[:, pl.ds(index, 1), :], sem_in.at[index]).start()
-        return carry
-
-    lax.fori_loop(0, padded, load, 0, unroll=4)
     place_of = jnp.sum(jnp.where(member, place_row + 1.0, 0.0), axis=1, keepdims=True) - 1.0
     rows_s[...] = dot_t((place_of == lane_c.astype(F32)).astype(F32), rows)[:padded]
 
@@ -610,6 +607,16 @@
     return out
 
 
+def spread(block, axis):
+    bit = lax.axis_size(axis) // 2
+    out = {0: block}
+    while bit:
+        pairs = [(i, i ^ bit) for i in range(lax.axis_size(axis))]
+        out.update({known | bit: lax.ppermute(out[known], axis, pairs) for known in sorted(out)})
+        bit //= 2
+    return [out[distance] for distance in sorted(out)]
+
+
 def body(crm_state, forcing, target, cost_class, level_map, remap_index, remap_weight):
     workers = lax.axis_size("crm")
     groups = lax.axis_size("grp")
@@ -622,9 +629,9 @@
     rows = pack(target, cost_class, forcing, level_map, workers, capacity)
     row_blocks = exchange([rows] * workers, "crm")
     fin, start, tendency, meta = run_models(row_blocks, in_hbm(crm_state.transpose(1, 0, 2)), levels)
-    tendencies = exchange([tendency] * workers, "crm")
+    tendencies = spread(tendency, "crm")
     water, clouds = condensate(workers, slots, cells, levels, meta, fin, tendency)
-    tendencies, clouds = lax.optimization_barrier((tendencies, clouds))
+    tendencies[2::2], clouds = lax.optimization_barrier((tendencies[2::2], clouds))
     clouds = exchange(clouds, "crm")
 
     edge = pl.pallas_call(

time: 34.7 us -> 34.5 us (level); the launches traced: 34.7 us -> 35 us
  Pallas kernels: 19.2 us -> 15.7 us
  starting transfers between devices: 7.57 us -> 9.92 us
  waiting for transfers between devices: 7.23 us -> 8.66 us
    ppermute x0 -> x3, waiting for transfers between devices: none -> 3.63 us  [spread(): lax.ppermute(out[known], axis, pairs)]
    pallas_call x1, Pallas kernels: 11.9 us -> 8.38 us  [run_models(): pl.pallas_call(functools.partial(model_kernel, workers, slots, levels, wi...]
    ppermute x1, starting transfers between devices: 0.64 us -> 4.09 us  [body(): edge = lax.ppermute(edge, ('grp', 'crm'), pairs)]
    ppermute x9 -> x6, starting transfers between devices: 6.92 us -> 5.11 us  [exchange(): lax.ppermute(blocks[distance], axis, [(i, i ^ distance) for i in range(si...]
    ppermute x1, waiting for transfers between devices: 3.11 us -> 2.01 us  [body(): edge = lax.ppermute(edge, ('grp', 'crm'), pairs)]
    ppermute x9 -> x6, waiting for transfers between devices: 4.12 us -> 3.03 us  [exchange(): lax.ppermute(blocks[distance], axis, [(i, i ^ distance) for i in range(si...]
    ppermute x0 -> x3, starting transfers between devices: none -> 0.71 us  [spread(): lax.ppermute(out[known], axis, pairs)]
where the time goes in v3:
time: 34.5 us; the launch traced here: 35 us
  Pallas kernels  15.7 us (46%)
  starting transfers between devices  9.92 us (29%)
  waiting for transfers between devices  8.66 us (25%)
  between operations  0.71 us (2%)
    pallas_call x1, Pallas kernels, run_models(): pl.pallas_call(functools.partial(model_kernel, workers, slots, levels, wi...  8.38 us
    ppermute x6, starting transfers between devices, exchange(): lax.ppermute(blocks[distance], axis, [(i, i ^ distance) for i in range(si...  5.11 us
    ppermute x1, starting transfers between devices, body(): edge = lax.ppermute(edge, ('grp', 'crm'), pairs)  4.09 us
    ppermute x3, waiting for transfers between devices, spread(): lax.ppermute(out[known], axis, pairs)  3.63 us
    ppermute x6, waiting for transfers between devices, exchange(): lax.ppermute(blocks[distance], axis, [(i, i ^ distance) for i in range(si...  3.03 us
    pallas_call x1, Pallas kernels, state_rows(): pl.pallas_call(functools.partial(state_kernel, slots, levels, width, colu...  2.67 us
    ppermute x1, waiting for transfers between devices, body(): edge = lax.ppermute(edge, ('grp', 'crm'), pairs)  2.01 us
    pallas_call x1, Pallas kernels, body(): pl.pallas_call(functools.partial(finish_kernel, columns, capacity, worker...  1.85 us
  transfers between devices with their start and end apart: 10, of which 6 were waited for; matrix products, arithmetic and copies ran while one was open for 0% of the time, Pallas kernels for 12%

profile of v3, /device:TPU:0, one launch (start us, length us, event | category | flops | bytes accessed | tf_op | source)
XLA Modules:
  0.0 35.0 jit_solution(9636002439469664489)
XLA Ops:
  0.6 1.1 %pack_forcing.1.refs_0_ = f32[24,128]{1,0:T(8,128)S(1)} custom-call(s32[24]{0:T(128)} %refs_0_.1, s32[24]{0:T(128)} %cost_hbm.1, f32[24,2,72]{2,1,0:T(2,128)} %forcing_hbm.1, f32[58,72]{1,0:T(8,128)} %refs_6_.1), custom_call_target="tpu_custom_call" | custom-call | tf_op jit(solution)/shard_map/pack_forcing/pallas_call | solution.py:96
  1.8 2.5 %collective-permute-start.2 = (f32[24,128]{1,0:T(8,128)S(1)}, f32[24,128]{1,0:T(8,128)S(1)}, u32[]{:S(2)}, u32[]{:S(2)}) collective-permute-start(f32[24,128]{1,0:T(8,128)S(1)} %pack_forcing.1.refs_0_), channel_id=1, source_target_pairs={{0,3},{1,2},{2,1},{3,0},{4,7},{5,6},{6,5},{7,4},{8,11},{9,10},{10,... | collective-permute-start | bytes 36872 | tf_op jit(solution)/shard_map/ppermute | solution.py:606
  4.3 0.6 %collective-permute-start.1 = (f32[24,128]{1,0:T(8,128)S(1)}, f32[24,128]{1,0:T(8,128)S(1)}, u32[]{:S(2)}, u32[]{:S(2)}) collective-permute-start(f32[24,128]{1,0:T(8,128)S(1)} %pack_forcing.1.refs_0_), channel_id=1, source_target_pairs={{0,2},{1,3},{2,0},{3,1},{4,6},{5,7},{6,4},{7,5},{8,10},{9,11},{10,... | collective-permute-start | bytes 36872 | tf_op jit(solution)/shard_map/ppermute | solution.py:606
  4.9 0.0 collective-permute-start
  4.9 0.7 %collective-permute-done.2.refs_3_ = f32[24,128]{1,0:T(8,128)S(1)} collective-permute-done((f32[24,128]{1,0:T(8,128)S(1)}, f32[24,128]{1,0:T(8,128)S(1)}, u32[]{:S(2)}, u32[]{:S(2)}) %collective-permute-start.2) | collective-permute-done | bytes 12320 | tf_op jit(solution)/shard_map/ppermute | solution.py:606
  5.7 2.3 %collective-permute-done.1.refs_2_ = f32[24,128]{1,0:T(8,128)S(1)} collective-permute-done((f32[24,128]{1,0:T(8,128)S(1)}, f32[24,128]{1,0:T(8,128)S(1)}, u32[]{:S(2)}, u32[]{:S(2)}) %collective-permute-start.1) | collective-permute-done | bytes 12320 | tf_op jit(solution)/shard_map/ppermute | solution.py:606
  8.0 0.0 collective-permute-done.refs_1_
  8.0 0.0 copy-start
  8.0 0.0 copy-start.1
  8.0 0.0 copy-start.2
  8.0 8.4 %cloud_models.1 = (f32[5,96,8,128]{3,2,1,0:T(8,128)S(1)}, f32[3,40,3712]{2,1,0:T(8,128)S(1)}, f32[40,128]{1,0:T(8,128)S(1)}, s32[8,128]{1,0:T(8,128)S(1)}) custom-call(f32[24,128]{1,0:T(8,128)S(1)} %pack_forcing.1.refs_0_, f32[24,128]{1,0:T(8,128)S(1)} %collective-permute-done.refs_1_, f32[24,128]{1,0:T(8,128)S(1)} %collective-permute-done.1.refs_2_, ...), custom_call_target="tpu_custom_call" | custom-call | bytes 41943040 | tf_op jit(solution)/shard_map/cloud_models/pallas_call | solution.py:447
  16.4 0.2 collective-permute-start.4
  16.6 1.2 %condensate.1 = (f32[40,3712]{1,0:T(8,128)S(1)}, f32[288,128]{1,0:T(8,128)S(1)}, f32[288,128]{1,0:T(8,128)S(1)}, f32[288,128]{1,0:T(8,128)S(1)}, f32[288,128]{1,0:T(8,128)S(1)}) custom-call(s32[8,128]{1,0:T(8,128)S(1)} %get-tuple-element.36.meta, f32[5,96,8,128]{3,2,1,0:T(8,128)S(1)} %get-tuple-element.30.fin, f32[40,128]{1,0:T(8,128)S(1)} %get-tuple-element.39.t_ref.refs_0_), custom_call_target="tpu_custom_call" | custom-call | bytes 8388608 | tf_op jit(solution)/shard_map/condensate/pallas_call | solution.py:478
  17.8 2.4 %collective-permute-done.4.refs_2_ = f32[40,128]{1,0:T(8,128)S(1)} collective-permute-done((f32[40,128]{1,0:T(8,128)S(1)}, f32[40,128]{1,0:T(8,128)S(1)}, u32[]{:S(2)}, u32[]{:S(2)}) %collective-permute-start.4) | collective-permute-done | bytes 20512 | tf_op jit(solution)/shard_map/ppermute | solution.py:615
  20.2 0.3 collective-permute-start.6
  20.5 1.6 %collective-permute-start.7 = (f32[288,128]{1,0:T(8,128)S(1)}, f32[288,128]{1,0:T(8,128)S(1)}, u32[]{:S(2)}, u32[]{:S(2)}) collective-permute-start(f32[288,128]{1,0:T(8,128)S(1)} %get-tuple-element.46), channel_id=1, source_target_pairs={{0,2},{1,3},{2,0},{3,1},{4,6},{5,7},{6,4},{7,5},{8,10},{9,11},{10,... | collective-permute-start | bytes 442376 | tf_op jit(solution)/shard_map/ppermute | solution.py:606
  22.2 0.0 collective-permute-start.8
  22.2 0.5 %collective-permute-start.3 = (f32[40,128]{1,0:T(8,128)S(1)}, f32[40,128]{1,0:T(8,128)S(1)}, u32[]{:S(2)}, u32[]{:S(2)}) collective-permute-start(f32[40,128]{1,0:T(8,128)S(1)} %get-tuple-element.39.t_ref.refs_0_), channel_id=1, source_target_pairs={{0,1},{1,0},{2,3},{3,2},{4,5},{5,4},{6,7},{7,6},{8,9},{9,8},{10,11... | collective-permute-start | bytes 61448 | tf_op jit(solution)/shard_map/ppermute | solution.py:615
  22.7 0.0 collective-permute-start.5
  22.7 0.8 %collective-permute-done.3.refs_1_ = f32[40,128]{1,0:T(8,128)S(1)} collective-permute-done((f32[40,128]{1,0:T(8,128)S(1)}, f32[40,128]{1,0:T(8,128)S(1)}, u32[]{:S(2)}, u32[]{:S(2)}) %collective-permute-start.3) | collective-permute-done | bytes 20512 | tf_op jit(solution)/shard_map/ppermute | solution.py:615
  23.5 0.3 collective-permute-done.5.refs_3_
  23.9 0.4 %edge_columns.1 = f32[24,128]{1,0:T(8,128)S(1)} custom-call(f32[40,128]{1,0:T(8,128)S(1)} %get-tuple-element.39.t_ref.refs_0_, f32[40,128]{1,0:T(8,128)S(1)} %collective-permute-done.3.refs_1_, f32[40,128]{1,0:T(8,128)S(1)} %collective-permute-done.4.refs_2_, f32[40,128]{1,0:T(8,128)S(1)} %collective-permute-done.5.refs_3_), custom_call_target="tpu_custom_call" | custom-call | bytes 1048576 | tf_op jit(solution)/shard_map/edge_columns/pallas_call | solution.py:637
  24.3 4.1 %collective-permute-start.9 = (f32[24,128]{1,0:T(8,128)S(1)}, f32[24,128]{1,0:T(8,128)S(1)}, u32[]{:S(2)}, u32[]{:S(2)}) collective-permute-start(f32[24,128]{1,0:T(8,128)S(1)} %edge_columns.1), channel_id=1, source_target_pairs={{0,4},{1,5},{6,2},{7,3},{4,8},{5,9},{10,6},{11,7},{8,12},{9,13},{1... | collective-permute-start | bytes 36872 | tf_op jit(solution)/shard_map/ppermute | solution.py:651
  28.4 0.0 copy-done
  28.4 0.0 copy-done.1
  28.4 0.0 copy-done.2
  28.4 0.0 copy-start.3
  28.4 2.7 %state_rows.1 = (f32[3,36,3712]{2,1,0:T(8,128)}, f32[24,128]{1,0:T(8,128)S(1)}, f32[2,128,72]{2,1,0:T(8,128)S(1)}) custom-call(s32[8,128]{1,0:T(8,128)S(1)} %get-tuple-element.36.meta, f32[5,96,8,128]{3,2,1,0:T(8,128)S(1)} %get-tuple-element.30.fin, f32[40,128]{1,0:T(8,128)S(1)} %get-tuple-element.39.t_ref.refs_0_, f32[40,3712]{1,0:T(8,128)S(1)} %get-tuple-element.37.water, ...), custom_call_target="tpu_custom_call" | custom-call | bytes 12582912 | tf_op jit(solution)/shard_map/state_rows/pallas_call | solution.py:495
  31.1 2.0 %collective-permute-done.9.refs_7_ = f32[24,128]{1,0:T(8,128)S(1)} collective-permute-done((f32[24,128]{1,0:T(8,128)S(1)}, f32[24,128]{1,0:T(8,128)S(1)}, u32[]{:S(2)}, u32[]{:S(2)}) %collective-permute-start.9) | collective-permute-done | bytes 12320 | tf_op jit(solution)/shard_map/ppermute | solution.py:651
  33.1 0.0 collective-permute-done.6.refs_2_
  33.1 0.0 collective-permute-done.7.refs_3_
  33.1 0.0 collective-permute-done.8.refs_4_
  33.1 0.0 copy-done.3
  33.1 1.8 %columns_out.1 = (f32[24,3712]{1,0:T(8,128)}, f32[24,2,72]{2,1,0:T(2,128)}) custom-call(s32[24]{0:T(128)S(1)} %copy-done.3, f32[288,128]{1,0:T(8,128)S(1)} %get-tuple-element.44.refs_1_, f32[288,128]{1,0:T(8,128)S(1)} %collective-permute-done.6.refs_2_, f32[288,128]{1,0:T(8,128)S(1)} %collective-permute-done.7.refs_3_, ...), custom_call_target="tpu_custom_call" | custom-call | bytes 1048576 | tf_op jit(solution)/shard_map/columns_out/pallas_call | solution.py:656
Async XLA Ops:
  1.8 3.9 %collective-permute-start.2 = (f32[24,128]{1,0:T(8,128)S(1)}, f32[24,128]{1,0:T(8,128)S(1)}, u32[]{:S(2)}, u32[]{:S(2)}) collective-permute-start(f32[24,128]{1,0:T(8,128)S(1)} %pack_forcing.1.refs_0_), channel_id=1, source_target_pairs={{0,3},{1,2},{2,1},{3,0},{4,7},{5,6},{6,5},{7,4},{8,11},{9,10},{10,... | collective-permute-start | bytes 36872 | tf_op jit(solution)/shard_map/ppermute | solution.py:606
  4.3 3.7 %collective-permute-start.1 = (f32[24,128]{1,0:T(8,128)S(1)}, f32[24,128]{1,0:T(8,128)S(1)}, u32[]{:S(2)}, u32[]{:S(2)}) collective-permute-start(f32[24,128]{1,0:T(8,128)S(1)} %pack_forcing.1.refs_0_), channel_id=1, source_target_pairs={{0,2},{1,3},{2,0},{3,1},{4,6},{5,7},{6,4},{7,5},{8,10},{9,11},{10,... | collective-permute-start | bytes 36872 | tf_op jit(solution)/shard_map/ppermute | solution.py:606
  4.9 3.1 %collective-permute-start = (f32[24,128]{1,0:T(8,128)S(1)}, f32[24,128]{1,0:T(8,128)S(1)}, u32[]{:S(2)}, u32[]{:S(2)}) collective-permute-start(f32[24,128]{1,0:T(8,128)S(1)} %pack_forcing.1.refs_0_), channel_id=1, source_target_pairs={{0,1},{1,0},{2,3},{3,2},{4,5},{5,4},{6,7},{7,6},{8,9},{9,8},{10,11... | collective-permute-start | bytes 36872 | tf_op jit(solution)/shard_map/ppermute | solution.py:606
  8.0 20.4 %copy-start = (f32[58,72]{1,0:T(8,128)S(1)}, f32[58,72]{1,0:T(8,128)}, u32[]{:S(2)}) copy-start(f32[58,72]{1,0:T(8,128)} %refs_6_.1) | copy-start | bytes 50116
  8.0 20.4 %copy-start.1 = (s32[24,4]{0,1:T(4,128)S(1)}, s32[24,4]{0,1:T(4,128)}, u32[]{:S(2)}) copy-start(s32[24,4]{0,1:T(4,128)} %param.12) | copy-start | bytes 1156
  8.0 20.4 %copy-start.2 = (f32[24,4]{0,1:T(4,128)S(1)}, f32[24,4]{0,1:T(4,128)}, u32[]{:S(2)}) copy-start(f32[24,4]{0,1:T(4,128)} %param.13) | copy-start | bytes 1156
  16.4 3.8 %collective-permute-start.4 = (f32[40,128]{1,0:T(8,128)S(1)}, f32[40,128]{1,0:T(8,128)S(1)}, u32[]{:S(2)}, u32[]{:S(2)}) collective-permute-start(f32[40,128]{1,0:T(8,128)S(1)} %get-tuple-element.39.t_ref.refs_0_), channel_id=1, source_target_pairs={{0,2},{1,3},{2,0},{3,1},{4,6},{5,7},{6,4},{7,5},{8,10},{9,11},{10,... | collective-permute-start | bytes 61448 | tf_op jit(solution)/shard_map/ppermute | solution.py:615
  20.2 12.9 %collective-permute-start.6 = (f32[288,128]{1,0:T(8,128)S(1)}, f32[288,128]{1,0:T(8,128)S(1)}, u32[]{:S(2)}, u32[]{:S(2)}) collective-permute-start(f32[288,128]{1,0:T(8,128)S(1)} %get-tuple-element.45), channel_id=1, source_target_pairs={{0,1},{1,0},{2,3},{3,2},{4,5},{5,4},{6,7},{7,6},{8,9},{9,8},{10,11... | collective-permute-start | bytes 442376 | tf_op jit(solution)/shard_map/ppermute | solution.py:606
  20.5 12.5 %collective-permute-start.7 = (f32[288,128]{1,0:T(8,128)S(1)}, f32[288,128]{1,0:T(8,128)S(1)}, u32[]{:S(2)}, u32[]{:S(2)}) collective-permute-start(f32[288,128]{1,0:T(8,128)S(1)} %get-tuple-element.46), channel_id=1, source_target_pairs={{0,2},{1,3},{2,0},{3,1},{4,6},{5,7},{6,4},{7,5},{8,10},{9,11},{10,... | collective-permute-start | bytes 442376 | tf_op jit(solution)/shard_map/ppermute | solution.py:606
  22.2 10.9 %collective-permute-start.8 = (f32[288,128]{1,0:T(8,128)S(1)}, f32[288,128]{1,0:T(8,128)S(1)}, u32[]{:S(2)}, u32[]{:S(2)}) collective-permute-start(f32[288,128]{1,0:T(8,128)S(1)} %get-tuple-element.47), channel_id=1, source_target_pairs={{0,3},{1,2},{2,1},{3,0},{4,7},{5,6},{6,5},{7,4},{8,11},{9,10},{10,... | collective-permute-start | bytes 442376 | tf_op jit(solution)/shard_map/ppermute | solution.py:606
  22.2 1.4 %collective-permute-start.3 = (f32[40,128]{1,0:T(8,128)S(1)}, f32[40,128]{1,0:T(8,128)S(1)}, u32[]{:S(2)}, u32[]{:S(2)}) collective-permute-start(f32[40,128]{1,0:T(8,128)S(1)} %get-tuple-element.39.t_ref.refs_0_), channel_id=1, source_target_pairs={{0,1},{1,0},{2,3},{3,2},{4,5},{5,4},{6,7},{7,6},{8,9},{9,8},{10,11... | collective-permute-start | bytes 61448 | tf_op jit(solution)/shard_map/ppermute | solution.py:615
  22.7 1.2 %collective-permute-start.5 = (f32[40,128]{1,0:T(8,128)S(1)}, f32[40,128]{1,0:T(8,128)S(1)}, u32[]{:S(2)}, u32[]{:S(2)}) collective-permute-start(f32[40,128]{1,0:T(8,128)S(1)} %collective-permute-done.4.refs_2_), channel_id=1, source_target_pairs={{0,1},{1,0},{2,3},{3,2},{4,5},{5,4},{6,7},{7,6},{8,9},{9,8},{10,11... | collective-permute-start | bytes 61448 | tf_op jit(solution)/shard_map/ppermute | solution.py:615
  24.3 8.8 %collective-permute-start.9 = (f32[24,128]{1,0:T(8,128)S(1)}, f32[24,128]{1,0:T(8,128)S(1)}, u32[]{:S(2)}, u32[]{:S(2)}) collective-permute-start(f32[24,128]{1,0:T(8,128)S(1)} %edge_columns.1), channel_id=1, source_target_pairs={{0,4},{1,5},{6,2},{7,3},{4,8},{5,9},{10,6},{11,7},{8,12},{9,13},{1... | collective-permute-start | bytes 36872 | tf_op jit(solution)/shard_map/ppermute | solution.py:651
  28.4 4.7 %copy-start.3 = (s32[24]{0:T(128)S(1)}, s32[24]{0:T(128)}, u32[]{:S(2)}) copy-start(s32[24]{0:T(128)} %refs_0_.1) | copy-start | bytes 292
